TPU v7x, 32 devices: a whole 2x2x4 slice. The times are simulated.
32 devices in a mesh: dp: 16 (over z, x, core), tensor: 2 (over y).
Axes of the slice: x: 2, y: 2, z: 4, core: 2. Of those that a mesh axis runs over, the one named last changes fastest.
Arguments:
- tokens: bfloat16 [8192, 1536], P(('dp', 'tensor')), may hold values from -6 to 6
- lengths: int32 [16, 4], P('dp'), may hold values from 1 to 256, 512 in all within a row
- first_gain: float32 [1536], replicated, may hold values from 0.25 to 1.75
- query_weight: bfloat16 [1536, 1536], P(None, 'tensor'), may hold values from -0.21875 to 0.21875
- key_weight: bfloat16 [1536, 768], P(None, 'tensor'), may hold values from -0.21875 to 0.21875
- value_weight: bfloat16 [1536, 768], P(None, 'tensor'), may hold values from -0.15625 to 0.15625
- output_weight: bfloat16 [1536, 1536], P('tensor'), may hold values from -0.875 to 0.875
- second_gain: float32 [1536], replicated, may hold values from 0.25 to 1.75
- gate_weight: bfloat16 [1536, 4096], P(None, 'tensor'), may hold values from -0.15625 to 0.15625
- up_weight: bfloat16 [1536, 4096], P(None, 'tensor'), may hold values from -0.15625 to 0.15625
- down_weight: bfloat16 [4096, 1536], P('tensor'), may hold values from -0.09375 to 0.09375
- out_cotangent: bfloat16 [8192, 1536], P(('dp', 'tensor')), may hold values from -6 to 6
Outputs:
- layer_out: bfloat16 [8192, 1536], P(('dp', 'tensor'))
- tokens_grad: float32 [8192, 1536], P(('dp', 'tensor'))
- first_gain_grad: float32 [1536], replicated
- query_grad: float32 [1536, 1536], P(None, 'tensor')
- key_grad: float32 [1536, 768], P(None, 'tensor')
- value_grad: float32 [1536, 768], P(None, 'tensor')
- output_grad: float32 [1536, 1536], P('tensor')
- second_gain_grad: float32 [1536], replicated
- gate_grad: float32 [1536, 4096], P(None, 'tensor')
- up_grad: float32 [1536, 4096], P(None, 'tensor')
- down_grad: float32 [4096, 1536], P('tensor')
- rms_values: float32 [3], replicated
Inputs may be any that keep to these rules, and one draw needn't show every extreme that they name: Each row holds the lengths of the 4 sequences of one index of dp in packing order, summing to 512, the largest exactly 256.
All inputs are finite; a program needn't handle non-finite values.
Results may differ from a plain program's by a relative error of at most 0.014.
The roundings to bfloat16 on the way count: a program that leaves them out, or rounds other values in their place, can miss the bound.
Values may be sent and summed in bfloat16 or wider, within the bound.
A program may use at most 320 MiB of HBM per device.

v0:
```python
import jax
import jax.numpy as jnp
from jax import lax
from jax.sharding import PartitionSpec as P

HD = 96


epsilon = 1e-05
rope_base = 10000.0
masked_score = -1e30
block_limit = 512


def product(left_side, right_side):
    return jnp.dot(left_side, right_side, preferred_element_type=jnp.float32)


def times_rows(left_side, right_side):
    return lax.dot_general(
        left_side, right_side, (((0,), (0,)), ((), ())), preferred_element_type=jnp.float32
    )


def times_cols(left_side, right_side):
    return lax.dot_general(
        left_side, right_side, (((1,), (1,)), ((), ())), preferred_element_type=jnp.float32
    )


def tables(lens_row, total_rows, half_size):
    seq_ends = jnp.cumsum(lens_row, dtype=jnp.int32)
    starts = seq_ends - lens_row
    places = jnp.arange(total_rows, dtype=jnp.int32)
    segment = jnp.sum(
        (places[:, None] >= seq_ends[None, :]).astype(jnp.int32), axis=1, dtype=jnp.int32
    )
    member = segment[:, None] == jnp.arange(lens_row.shape[0], dtype=jnp.int32)[None, :]
    position = places - jnp.sum(jnp.where(member, starts[None, :], 0), axis=1, dtype=jnp.int32)
    inverse = rope_base ** (-2.0 * jnp.arange(half_size, dtype=jnp.float32) / (2 * half_size))
    angles = position.astype(jnp.float32)[:, None] * inverse[None, :]
    return (places, segment, jnp.cos(angles), jnp.sin(angles))


def rotate(values, cosine_table, sine_table, direction):
    total_rows = values.shape[0]
    half_size = cosine_table.shape[1]
    shaped = values.reshape(total_rows, -1, 2 * half_size)
    first_half = shaped[..., :half_size]
    second = shaped[..., half_size:]
    cos_b = cosine_table[:, None, :]
    sin_b = sine_table[:, None, :] * direction
    turned = jnp.concatenate(
        [first_half * cos_b - second * sin_b, second * cos_b + first_half * sin_b], axis=-1
    )
    return turned.reshape(total_rows, -1)


def norm_rows(values, gain):
    inv_rms = lax.rsqrt(jnp.mean(values * values, axis=-1, keepdims=True) + epsilon)
    return (values * inv_rms * gain, inv_rms)


def norm_back(values, inv_rms, gain, upstream):
    scaled = upstream * gain
    row_inner = jnp.mean(scaled * values, axis=-1, keepdims=True)
    gain_rows = jnp.sum(upstream * values * inv_rms, axis=0)
    return (gain_rows, inv_rms * (scaled - values * inv_rms * inv_rms * row_inner))


def body(
    tokens,
    lengths,
    first_gain,
    query_weight,
    key_weight,
    value_weight,
    output_weight,
    second_gain,
    gate_weight,
    up_weight,
    down_weight,
    out_cotangent,
):
    inputs = tokens.astype(jnp.float32)
    normed1, inv_first = norm_rows(inputs, first_gain)
    normed1 = normed1.astype(jnp.bfloat16)
    full_first = lax.all_gather(normed1, "tensor", axis=0, tiled=True)
    total_rows = full_first.shape[0]
    places, segment, cosine_table, sine_table = tables(lengths[0], total_rows, HD // 2)
    kv_heads = key_weight.shape[1] // HD
    groups = query_weight.shape[1] // key_weight.shape[1]
    query = rotate(product(full_first, query_weight), cosine_table, sine_table, 1.0).astype(
        jnp.bfloat16
    )
    keys = rotate(product(full_first, key_weight), cosine_table, sine_table, 1.0).astype(
        jnp.bfloat16
    )
    values = product(full_first, value_weight).astype(jnp.bfloat16)
    block_rows = min(block_limit, total_rows)
    block_count = total_rows // block_rows
    query_blocks = query.reshape(block_count, block_rows, kv_heads, groups, HD)
    seg_blocks = segment.reshape(block_count, block_rows)
    place_blocks = places.reshape(block_count, block_rows)
    key_three = keys.reshape(total_rows, kv_heads, HD)
    value_three = values.reshape(total_rows, kv_heads, HD)
    factor = HD ** (-0.5)

    def scores(query_block, seg_block, place_block):
        raw = (
            jnp.einsum("qcgd,kcd->cgqk", query_block, key_three, preferred_element_type=jnp.float32)
            * factor
        )
        allowed = (seg_block[:, None] == segment[None, :]) & (
            place_block[:, None] >= places[None, :]
        )
        return (jnp.where(allowed[None, None], raw, masked_score), allowed)

    def forward_block(piece_set):
        query_block, seg_block, place_block = piece_set
        masked, allowed = scores(query_block, seg_block, place_block)
        highest = jnp.max(masked, axis=-1, keepdims=True)
        exponent = jnp.exp(masked - highest)
        denominator = jnp.sum(exponent, axis=-1, keepdims=True)
        weights = exponent / denominator
        output = jnp.einsum(
            "cgqk,kcd->qcgd",
            weights.astype(jnp.bfloat16),
            value_three,
            preferred_element_type=jnp.float32,
        )
        stored = (highest + jnp.log(denominator))[..., 0]
        return (output.reshape(block_rows, -1), stored)

    out_blocks, kept_blocks = lax.map(forward_block, (query_blocks, seg_blocks, place_blocks))
    attended = out_blocks.reshape(total_rows, -1).astype(jnp.bfloat16)
    attn_rows = lax.psum_scatter(
        product(attended, output_weight), "tensor", scatter_dimension=0, tiled=True
    )
    middle = inputs + attn_rows
    normed2, inv_second = norm_rows(middle, second_gain)
    normed2 = normed2.astype(jnp.bfloat16)
    full_second = lax.all_gather(normed2, "tensor", axis=0, tiled=True)
    gate_value = product(full_second, gate_weight)
    upward = product(full_second, up_weight)
    gate_sig = jax.nn.sigmoid(gate_value)
    hidden = (gate_value * gate_sig * upward).astype(jnp.bfloat16)
    mlp_rows = lax.psum_scatter(
        product(hidden, down_weight), "tensor", scatter_dimension=0, tiled=True
    )
    layer_out = middle + mlp_rows
    squares = jnp.stack(
        [
            jnp.sum(layer_out * layer_out),
            jnp.sum(attn_rows * attn_rows),
            jnp.sum(mlp_rows * mlp_rows),
        ]
    )
    grad_full = lax.all_gather(out_cotangent, "tensor", axis=0, tiled=True)
    grad_hidden = times_cols(grad_full, down_weight)
    down_g = times_rows(hidden, grad_full)
    gate_slope = gate_sig * (1.0 + gate_value * (1.0 - gate_sig))
    grad_gate = (grad_hidden * upward * gate_slope).astype(jnp.bfloat16)
    grad_up = (grad_hidden * gate_value * gate_sig).astype(jnp.bfloat16)
    gate_g = times_rows(full_second, grad_gate)
    up_g = times_rows(full_second, grad_up)
    gate_g, up_g, down_g = lax.psum((gate_g, up_g, down_g), "dp")
    grad_normed2 = lax.psum_scatter(
        times_cols(grad_gate, gate_weight) + times_cols(grad_up, up_weight),
        "tensor",
        scatter_dimension=0,
        tiled=True,
    )
    second_rows, grad_mid_norm = norm_back(middle, inv_second, second_gain, grad_normed2)
    grad_middle = out_cotangent.astype(jnp.float32) + grad_mid_norm
    grad_attn_full = lax.all_gather(grad_middle.astype(jnp.bfloat16), "tensor", axis=0, tiled=True)
    output_g = times_rows(attended, grad_attn_full)
    grad_out = times_cols(grad_attn_full, output_weight).astype(jnp.bfloat16)
    grad_blocks = grad_out.reshape(block_count, block_rows, kv_heads, groups, HD)

    def backward_block(running, piece_set):
        key_acc, value_acc = running
        query_block, seg_block, place_block, grad_block, stored = piece_set
        masked, allowed = scores(query_block, seg_block, place_block)
        weights = jnp.where(allowed[None, None], jnp.exp(masked - stored[..., None]), 0.0)
        grad_weights = jnp.einsum(
            "qcgd,kcd->cgqk", grad_block, value_three, preferred_element_type=jnp.float32
        )
        row_inner = jnp.sum(weights * grad_weights, axis=-1, keepdims=True)
        grad_scores = (weights * (grad_weights - row_inner)).astype(jnp.bfloat16)
        grad_query = (
            jnp.einsum("cgqk,kcd->qcgd", grad_scores, key_three, preferred_element_type=jnp.float32)
            * factor
        )
        key_acc = (
            key_acc
            + jnp.einsum(
                "cgqk,qcgd->kcd", grad_scores, query_block, preferred_element_type=jnp.float32
            )
            * factor
        )
        value_acc = value_acc + jnp.einsum(
            "cgqk,qcgd->kcd",
            weights.astype(jnp.bfloat16),
            grad_block,
            preferred_element_type=jnp.float32,
        )
        return ((key_acc, value_acc), grad_query.reshape(block_rows, -1))

    zeros_kv = jnp.zeros((total_rows, kv_heads, HD), jnp.float32)
    (key_rot_grad, value_acc_grad), query_rot_grad = lax.scan(
        backward_block,
        (zeros_kv, zeros_kv),
        (query_blocks, seg_blocks, place_blocks, grad_blocks, kept_blocks),
    )
    query_lin = rotate(
        query_rot_grad.reshape(total_rows, -1), cosine_table, sine_table, -1.0
    ).astype(jnp.bfloat16)
    key_lin = rotate(key_rot_grad.reshape(total_rows, -1), cosine_table, sine_table, -1.0).astype(
        jnp.bfloat16
    )
    value_lin = value_acc_grad.reshape(total_rows, -1).astype(jnp.bfloat16)
    query_g = times_rows(full_first, query_lin)
    key_g = times_rows(full_first, key_lin)
    value_g = times_rows(full_first, value_lin)
    grad_normed1 = lax.psum_scatter(
        times_cols(query_lin, query_weight)
        + times_cols(key_lin, key_weight)
        + times_cols(value_lin, value_weight),
        "tensor",
        scatter_dimension=0,
        tiled=True,
    )
    first_rows, grad_in_norm = norm_back(inputs, inv_first, first_gain, grad_normed1)
    tokens_grad = grad_middle + grad_in_norm
    gain_rows = jnp.stack([first_rows, second_rows])
    query_g, key_g, value_g, output_g, gain_rows, squares = lax.psum(
        (query_g, key_g, value_g, output_g, gain_rows, squares), "dp"
    )
    gain_rows, squares = lax.psum((gain_rows, squares), "tensor")
    rms_values = jnp.sqrt(squares / (total_rows * lax.axis_size("dp")))
    return (
        layer_out.astype(jnp.bfloat16),
        tokens_grad,
        gain_rows[0],
        query_g,
        key_g,
        value_g,
        output_g,
        gain_rows[1],
        gate_g,
        up_g,
        down_g,
        rms_values,
    )


def solution(mesh):
    in_specs = (
        P(("dp", "tensor"), None),
        P("dp", None),
        P(),
        P(None, "tensor"),
        P(None, "tensor"),
        P(None, "tensor"),
        P("tensor", None),
        P(),
        P(None, "tensor"),
        P(None, "tensor"),
        P("tensor", None),
        P(("dp", "tensor"), None),
    )
    out_specs = (
        P(("dp", "tensor"), None),
        P(("dp", "tensor"), None),
        P(),
        P(None, "tensor"),
        P(None, "tensor"),
        P(None, "tensor"),
        P("tensor", None),
        P(),
        P(None, "tensor"),
        P(None, "tensor"),
        P("tensor", None),
        P(),
    )
    return jax.shard_map(body, mesh=mesh, in_specs=in_specs, out_specs=out_specs, check_vma=False)
```

profile of v0, /device:TPU:0, one launch (start us, length us, event | category | flops | bytes accessed | tf_op | source)
XLA Modules:
  0.0 1308.3 jit_solution(17890817246827183314)
XLA Ops:
  7.3 1.5 fusion.18
  8.8 2.3 fusion.13
  12.8 28.3 %all-gather.5.cloned.1.call-done = bf16[512,1536]{1,0:T(8,128)(2,1)} async-done(((bf16[256,1536]{1,0:T(8,128)(2,1)}), bf16[512,1536]{1,0:T(8,128)(2,1)}) %all-gather.5.cloned.1.call-update) | async-done | bytes 1572880 | tf_op jit(solution)/shard_map/all_gather | solution.py:88
  41.1 2.7 fusion.38
  45.9 1.7 fusion.37
  51.0 1.7 fusion.22
  53.6 3.1 fusion.40
  56.8 43.4 %reduce-scatter.5.cloned.1.call-done = f32[256,1536]{1,0:T(8,128)} async-done(((f32[512,1536]{1,0:T(8,128)}), f32[256,1536]{1,0:T(8,128)}) %reduce-scatter.5.cloned.1.call-update) | async-done | bytes 1572880 | tf_op jit(solution)/shard_map/reduce_scatter | solution.py:137
  100.2 2.5 multiply_reduce_fusion.5
  105.9 26.5 %all-gather.7.cloned.1.call-done = bf16[512,1536]{1,0:T(8,128)(2,1)} async-done(((bf16[256,1536]{1,0:T(8,128)(2,1)}), bf16[512,1536]{1,0:T(8,128)(2,1)}) %all-gather.7.cloned.1.call-update) | async-done | bytes 1572880 | tf_op jit(solution)/shard_map/all_gather | solution.py:143
  132.3 8.8 fusion.42
  141.2 8.2 fusion.41
  149.3 11.7 all-gather.9.cloned.1.call-done
  161.1 11.7 multiply_convert_fusion
  172.7 7.3 fusion.44
  180.0 8.0 convolution_add_fusion.2
  188.1 9.7 reduce-scatter.7.cloned.1.call-start
  197.8 8.5 fusion.43
  206.4 25.2 %reduce-scatter.9.cloned.1.call-done = f32[256,1536]{1,0:T(8,128)} async-done(((f32[512,1536]{1,0:T(8,128)}), f32[256,1536]{1,0:T(8,128)}) %reduce-scatter.9.cloned.1.call-update) | async-done | bytes 1572880 | tf_op jit(solution)/shard_map/reduce_scatter | solution.py:168
  231.6 46.1 %reduce-scatter.7.cloned.1.call-done = f32[256,1536]{1,0:T(8,128)} async-done(((f32[512,1536]{1,0:T(8,128)}), f32[256,1536]{1,0:T(8,128)}) %reduce-scatter.7.cloned.1.call-update) | async-done | bytes 1572880 | tf_op jit(solution)/shard_map/reduce_scatter | solution.py:148
  277.7 5.0 multiply_reduce_fusion.2
  284.9 26.6 %all-gather.11.cloned.1.call-done = bf16[512,1536]{1,0:T(8,128)(2,1)} async-done(((bf16[256,1536]{1,0:T(8,128)(2,1)}), bf16[512,1536]{1,0:T(8,128)(2,1)}) %all-gather.11.cloned.1.call-update) | async-done | bytes 1572880 | tf_op jit(solution)/shard_map/all_gather | solution.py:176
  311.5 3.7 convolution_convert_fusion
  316.6 5.1 fusion.28
  321.7 5.2 fusion
  326.9 2.6 fusion.2
  332.4 1.6 copy-done.44
  336.8 2.7 convolution_add_fusion
  339.8 10.4 fusion.52
  350.3 6.6 fusion.51
  356.9 6.6 fusion.50
  363.5 2.4 fusion.48
  366.0 2.4 fusion.47
  368.4 3.6 fusion.49
  372.0 3.6 fusion.46
  375.7 2.2 pad_maximum_fusion.4
  377.9 5.1 reduce-scatter.11.cloned.1.call-done
  383.0 1.8 fusion.21
  384.9 64.5 %all-reduce = (f32[2,1536]{1,0:T(2,128)S(1)}, f32[3]{0:T(128)S(1)}) all-reduce(f32[2,1536]{1,0:T(2,128)S(1)} %pad_maximum_fusion.3, f32[3]{0:T(128)S(1)} %pad_maximum_fusion.4), channel_id=1, replica_groups=mesh['dp'=16,'tensor'=2] {'dp'}, use_global_device_ids=true, to_apply=%region_16.17 | all-reduce | flops 3075 | bytes 24600 | tf_op jit(solution)/shard_map/psum | solution.py:237
  449.3 7.1 all-reduce.2
  457.6 4.3 fusion.17
  461.9 792.6 %all-reduce.5.cloned.1.call-done = (f32[1536,768]{1,0:T(8,128)}, f32[1536,384]{1,0:T(8,128)}, f32[1536,384]{1,0:T(8,128)}, f32[768,1536]{1,0:T(8,128)}, f32[1536...) async-done(((f32[1536,768]{1,0:T(8,128)}, f32[1536,384]{1,0:T(8,128)}, f32[1536,384]{1,0:T(8,128)}, f32[768,1536]{1,0:T(8,128)}, f32[1536,2048]{1,0:T(8,128)}, ...) | async-done | bytes 51904528 | tf_op jit(solution)/shard_map/psum | solution.py:237
  1254.6 5.0 copy.64
  1263.5 1.8 copy-done.14
  1265.3 2.2 copy.67
  1267.4 11.5 copy.68
  1279.0 11.5 copy.69
  1290.5 10.8 copy.70
  (163 shorter events, 25.9 us)
Async XLA Ops:
  7.2 46.4 %copy-start = (bf16[768,1536]{1,0:T(8,128)(2,1)S(1)}, bf16[768,1536]{1,0:T(8,128)(2,1)}, u32[]{:S(2)}) copy-start(bf16[768,1536]{1,0:T(8,128)(2,1)} %param.18) | copy-start | bytes 7077892
  7.2 3.9 copy-start.48
  7.2 33.9 %all-gather.5.cloned.1.call-start = ((), (), s32[]{:S(2)}) async-start(), calls=%async_computation.4 | async-start | bytes 2359296 | tf_op jit(solution)/shard_map/all_gather | solution.py:88
  8.8 2.6 copy-start.39
  11.1 89.1 %reduce-scatter.5.cloned.1.call-start = ((), (), s32[]{:S(2)}) async-start(), calls=%async_computation.5 | async-start | bytes 4718592 | tf_op jit(solution)/shard_map/reduce_scatter | solution.py:137
  41.1 2.9 copy-start.6
  41.1 3.0 copy-start.43
  47.6 3.4 copy-start.2
  49.8 2.9 copy-start.36
  56.7 43.5 %copy-start.8 = (bf16[256,1536]{1,0:T(8,128)(2,1)S(1)}, bf16[256,1536]{1,0:T(8,128)(2,1)}, u32[]{:S(2)}) copy-start(bf16[256,1536]{1,0:T(8,128)(2,1)} %param.12) | copy-start | bytes 2359300
  56.7 47.2 %copy-start.34 = (f32[1536]{0:T(1024)S(1)}, f32[1536]{0:T(1024)}, u32[]{:S(2)}) copy-start(f32[1536]{0:T(1024)} %param.19) | copy-start | bytes 18436
  56.7 75.6 %all-gather.7.cloned.1.call-start = ((), (), s32[]{:S(2)}) async-start(), calls=%async_computation.6 | async-start | bytes 2359296 | tf_op jit(solution)/shard_map/all_gather | solution.py:143
  102.7 179.9 %copy-start.37 = (f32[256]{0:T(256)}, f32[256]{0:T(256)S(1)}, u32[]{:S(2)}) copy-start(f32[256]{0:T(256)S(1)} %add_rsqrt_fusion) | copy-start | bytes 3076
  105.0 56.1 %all-gather.9.cloned.1.call-start = ((), (), s32[]{:S(2)}) async-start(), calls=%async_computation.8 | async-start | bytes 2359296 | tf_op jit(solution)/shard_map/all_gather | solution.py:159
  105.6 126.0 %reduce-scatter.9.cloned.1.call-start = ((), (), s32[]{:S(2)}) async-start(), calls=%async_computation.9 | async-start | bytes 4718592 | tf_op jit(solution)/shard_map/reduce_scatter | solution.py:168
  132.3 8.8 copy-start.45
  172.7 7.3 copy-start.49
  172.7 7.3 copy-start.51
  188.1 89.6 %reduce-scatter.7.cloned.1.call-start = ((), (), s32[]{:S(2)}) async-start(), calls=%async_computation.7 | async-start | bytes 4718592 | tf_op jit(solution)/shard_map/reduce_scatter | solution.py:148
  206.3 105.1 %all-gather.11.cloned.1.call-start = ((), (), s32[]{:S(2)}) async-start(), calls=%async_computation.10 | async-start | bytes 2359296 | tf_op jit(solution)/shard_map/all_gather | solution.py:176
  277.7 5.0 copy-start.4
  277.7 5.0 copy-start.9
  277.7 5.0 copy-start.12
  284.1 98.9 %reduce-scatter.11.cloned.1.call-start = ((), (), s32[]{:S(2)}) async-start(), calls=%async_computation.11 | async-start | bytes 4718592 | tf_op jit(solution)/shard_map/reduce_scatter | solution.py:226
  316.6 5.1 copy-start.32
  316.6 10.3 slice-start
  321.7 14.9 %copy-start.26 = (bf16[4,96,512]{2,1,0:T(8,128)(2,1)}, bf16[4,96,512]{2,1,0:T(8,128)(2,1)S(1)}, u32[]{:S(2)}) copy-start(bf16[4,96,512]{2,1,0:T(8,128)(2,1)S(1)} %fusion.28) | copy-start | bytes 1179652
  321.7 5.2 slice-start.1
  326.9 2.6 copy-start.11
  332.4 3.1 copy-start.17
  339.5 10.7 copy-start.46
  339.5 915.1 %all-reduce.5.cloned.1.call-start = ((), (), s32[]{:S(2)}) async-start(), calls=%async_computation.12 | async-start | bytes 103809024 | tf_op jit(solution)/shard_map/psum | solution.py:237
  339.8 10.5 copy-start.52
  350.2 6.6 copy-start.47
  350.2 6.6 copy-start.50
  356.9 6.6 copy-start.7
  356.9 6.6 copy-start.27
  368.4 3.6 copy-start.18
  375.6 7.4 copy-start.35
  375.6 7.4 copy-start.40
  375.6 82.0 %copy-start.5 = (f32[256,1536]{1,0:T(8,128)S(1)}, f32[256,1536]{1,0:T(8,128)}, u32[]{:S(2)}) copy-start(f32[256,1536]{1,0:T(8,128)} %copy-done.3) | copy-start | bytes 4718596
  375.6 82.0 %copy-start.13 = (bf16[256,1536]{1,0:T(8,128)(2,1)S(1)}, bf16[256,1536]{1,0:T(8,128)(2,1)}, u32[]{:S(2)}) copy-start(bf16[256,1536]{1,0:T(8,128)(2,1)} %param.23) | copy-start | bytes 2359300
  375.7 82.0 %copy-start.38 = (f32[256]{0:T(256)S(1)}, f32[256]{0:T(256)}, u32[]{:S(2)}) copy-start(f32[256]{0:T(256)} %copy-done.37) | copy-start | bytes 3076
  375.7 82.0 %copy-start.42 = (f32[256]{0:T(256)S(1)}, f32[256]{0:T(256)}, u32[]{:S(2)}) copy-start(f32[256]{0:T(256)} %copy-done.41) | copy-start | bytes 3076
  1254.6 5.0 copy-start.20
  1259.6 2.5 copy-start.19
  1262.1 3.2 copy-start.14
  1290.5 10.8 copy-start.1
  (16 other events, 26.3 us)
Sparse Core Ops, SparseCore 0:
  11.2 29.8 all-gather.4
  56.8 43.3 reduce-scatter.4
  105.1 27.1 all-gather.6
  133.8 27.2 all-gather.8
  188.2 43.3 reduce-scatter.8
  234.3 43.3 reduce-scatter.6
  284.2 27.1 all-gather.10
  339.6 43.3 reduce-scatter.10
  390.1 864.4 all-reduce.4
where the time goes:
time: 1320 us; the launch traced here: 1310 us
  waiting for transfers between devices  1010 us (77%)
  matrix products  121 us (9%)
  blocking collectives  71.6 us (5%)
  local copies, waits for them, and re-layouts  54.3 us (4%)
  other arithmetic  29.7 us (2%)
  between operations  14.9 us (1%)
    psum x1, waiting for transfers between devices, body(): lax.psum((query_g, key_g, value_g, output_g, gain_rows, squares), 'dp')  793 us
    psum x1, blocking collectives, body(): lax.psum((query_g, key_g, value_g, output_g, gain_rows, squares), 'dp')  64.5 us
    unnamed x117, local copies, waits for them, and re-layouts  52.3 us
    reduce_scatter x1, waiting for transfers between devices, body(): lax.psum_scatter(product(hidden, down_weight), 'tensor', scatter_dimensio...  46.1 us
    reduce_scatter x1, waiting for transfers between devices, body(): lax.psum_scatter(product(attended, output_weight), 'tensor', scatter_dime...  43.4 us
    dot_general x7, matrix products, times_cols(): lax.dot_general(left_side, right_side, (((1,), (1,)), ((), ())), preferre...  35.9 us
    dot_general x7, matrix products, times_rows(): lax.dot_general(left_side, right_side, (((0,), (0,)), ((), ())), preferre...  35.7 us
    dot_general x7, matrix products, product(): return jnp.dot(left_side, right_side, preferred_element_type=jnp.float32)  33.5 us
  transfers between devices with their start and end apart: 9, of which 9 were waited for; matrix products, arithmetic and copies ran while one was open for 6% of the time, Pallas kernels for 0%

commit v1 on v0

--- a/solution.py
+++ b/solution.py
@@ -29,7 +29,9 @@
 
 
 def tables(lens_row, total_rows, half_size):
-    seq_ends = jnp.cumsum(lens_row, dtype=jnp.int32)
+    count = lens_row.shape[0]
+    earlier = jnp.arange(count)[:, None] <= jnp.arange(count)[None, :]
+    seq_ends = jnp.sum(jnp.where(earlier, lens_row[:, None], 0), axis=0, dtype=jnp.int32)
     starts = seq_ends - lens_row
     places = jnp.arange(total_rows, dtype=jnp.int32)
     segment = jnp.sum(
@@ -66,6 +68,17 @@
     row_inner = jnp.mean(scaled * values, axis=-1, keepdims=True)
     gain_rows = jnp.sum(upstream * values * inv_rms, axis=0)
     return (gain_rows, inv_rms * (scaled - values * inv_rms * inv_rms * row_inner))
+
+
+def dp_sum(terms):
+    low = lax.psum(tuple(term.astype(jnp.bfloat16) for term in terms), "dp")
+    return tuple(term.astype(jnp.float32) for term in low)
+
+
+def low_scatter(partial):
+    return lax.psum_scatter(
+        partial.astype(jnp.bfloat16), "tensor", scatter_dimension=0, tiled=True
+    ).astype(jnp.float32)
 
 
 def body(
@@ -134,9 +147,7 @@
 
     out_blocks, kept_blocks = lax.map(forward_block, (query_blocks, seg_blocks, place_blocks))
     attended = out_blocks.reshape(total_rows, -1).astype(jnp.bfloat16)
-    attn_rows = lax.psum_scatter(
-        product(attended, output_weight), "tensor", scatter_dimension=0, tiled=True
-    )
+    attn_rows = low_scatter(product(attended, output_weight))
     middle = inputs + attn_rows
     normed2, inv_second = norm_rows(middle, second_gain)
     normed2 = normed2.astype(jnp.bfloat16)
@@ -145,9 +156,7 @@
     upward = product(full_second, up_weight)
     gate_sig = jax.nn.sigmoid(gate_value)
     hidden = (gate_value * gate_sig * upward).astype(jnp.bfloat16)
-    mlp_rows = lax.psum_scatter(
-        product(hidden, down_weight), "tensor", scatter_dimension=0, tiled=True
-    )
+    mlp_rows = low_scatter(product(hidden, down_weight))
     layer_out = middle + mlp_rows
     squares = jnp.stack(
         [
@@ -164,12 +173,9 @@
     grad_up = (grad_hidden * gate_value * gate_sig).astype(jnp.bfloat16)
     gate_g = times_rows(full_second, grad_gate)
     up_g = times_rows(full_second, grad_up)
-    gate_g, up_g, down_g = lax.psum((gate_g, up_g, down_g), "dp")
-    grad_normed2 = lax.psum_scatter(
-        times_cols(grad_gate, gate_weight) + times_cols(grad_up, up_weight),
-        "tensor",
-        scatter_dimension=0,
-        tiled=True,
+    gate_g, up_g, down_g = dp_sum((gate_g, up_g, down_g))
+    grad_normed2 = low_scatter(
+        times_cols(grad_gate, gate_weight) + times_cols(grad_up, up_weight)
     )
     second_rows, grad_mid_norm = norm_back(middle, inv_second, second_gain, grad_normed2)
     grad_middle = out_cotangent.astype(jnp.float32) + grad_mid_norm
@@ -223,21 +229,16 @@
     query_g = times_rows(full_first, query_lin)
     key_g = times_rows(full_first, key_lin)
     value_g = times_rows(full_first, value_lin)
-    grad_normed1 = lax.psum_scatter(
+    grad_normed1 = low_scatter(
         times_cols(query_lin, query_weight)
         + times_cols(key_lin, key_weight)
-        + times_cols(value_lin, value_weight),
-        "tensor",
-        scatter_dimension=0,
-        tiled=True,
+        + times_cols(value_lin, value_weight)
     )
     first_rows, grad_in_norm = norm_back(inputs, inv_first, first_gain, grad_normed1)
     tokens_grad = grad_middle + grad_in_norm
     gain_rows = jnp.stack([first_rows, second_rows])
-    query_g, key_g, value_g, output_g, gain_rows, squares = lax.psum(
-        (query_g, key_g, value_g, output_g, gain_rows, squares), "dp"
-    )
-    gain_rows, squares = lax.psum((gain_rows, squares), "tensor")
+    query_g, key_g, value_g, output_g = dp_sum((query_g, key_g, value_g, output_g))
+    gain_rows, squares = lax.psum((gain_rows, squares), ("dp", "tensor"))
     rms_values = jnp.sqrt(squares / (total_rows * lax.axis_size("dp")))
     return (
         layer_out.astype(jnp.bfloat16),

time: 1320 us -> 822 us (0.62)
  waiting for transfers between devices: 1010 us -> 580 us
  local copies, waits for them, and re-layouts: 54.3 us -> 7.52 us
  blocking collectives: 71.6 us -> 41.7 us
  other arithmetic: 29.7 us -> 57.8 us
    psum x1, waiting for transfers between devices: 793 us -> 413 us  [dp_sum(): low = lax.psum(tuple((term.astype(jnp.bfloat16) for term in terms)), 'dp')]
    reduce_scatter x4, waiting for transfers between devices: 120 us -> 72.9 us  [low_scatter(): lax.psum_scatter(partial.astype(jnp.bfloat16), 'tensor', scatter_dimensio...]
    unnamed x117 -> x120, local copies, waits for them, and re-layouts: 52.3 us -> 5.47 us
    convert_element_type x0 -> x7, other arithmetic: none -> 30.6 us  [dp_sum(): return tuple((term.astype(jnp.float32) for term in low))]
    psum x2 -> x1, blocking collectives: 71.6 us -> 41.7 us  [body(): gain_rows, squares = lax.psum((gain_rows, squares), ('dp', 'tensor'))]
  transfers between devices with their start and end apart: 9 -> 9, of which waited for: 9 -> 8; matrix products, arithmetic and copies ran while one was open for 6% -> 8% of each run, Pallas kernels for 0% -> 0%
where the time goes in v1:
time: 822 us; the launch traced here: 814 us
  waiting for transfers between devices  580 us (71%)
  matrix products  111 us (14%)
  other arithmetic  57.8 us (7%)
  blocking collectives  41.7 us (5%)
  between operations  15 us (2%)
    psum x1, waiting for transfers between devices, dp_sum(): low = lax.psum(tuple((term.astype(jnp.bfloat16) for term in terms)), 'dp')  413 us
    reduce_scatter x4, waiting for transfers between devices, low_scatter(): lax.psum_scatter(partial.astype(jnp.bfloat16), 'tensor', scatter_dimensio...  72.9 us
    psum x1, blocking collectives, body(): gain_rows, squares = lax.psum((gain_rows, squares), ('dp', 'tensor'))  41.7 us
    dot_general x7, matrix products, times_cols(): lax.dot_general(left_side, right_side, (((1,), (1,)), ((), ())), preferre...  35 us
    dot_general x7, matrix products, product(): return jnp.dot(left_side, right_side, preferred_element_type=jnp.float32)  32.9 us
    convert_element_type x7, other arithmetic, dp_sum(): return tuple((term.astype(jnp.float32) for term in low))  30.6 us
    all_gather x1, waiting for transfers between devices, body(): full_first = lax.all_gather(normed1, 'tensor', axis=0, tiled=True)  28.4 us
    dot_general x7, matrix products, times_rows(): lax.dot_general(left_side, right_side, (((0,), (0,)), ((), ())), preferre...  27.5 us
  transfers between devices with their start and end apart: 9, of which 8 were waited for; matrix products, arithmetic and copies ran while one was open for 8% of the time, Pallas kernels for 0%

profile of v1, /device:TPU:0, one launch (start us, length us, event | category | flops | bytes accessed | tf_op | source)
XLA Modules:
  0.0 813.9 jit_solution(16417667073358583002)
XLA Ops:
  7.3 1.5 fusion.29
  8.8 2.3 fusion.18
  12.7 28.4 %all-gather.5.cloned.1.call-done = bf16[512,1536]{1,0:T(8,128)(2,1)} async-done(((bf16[256,1536]{1,0:T(8,128)(2,1)}), bf16[512,1536]{1,0:T(8,128)(2,1)}) %all-gather.5.cloned.1.call-update) | async-done | bytes 1572880 | tf_op jit(solution)/shard_map/all_gather | solution.py:101
  41.1 3.7 fusion.51
  47.2 1.7 fusion.49
  52.3 1.6 fusion.33
  54.8 2.6 convolution_convert_fusion.6
  57.5 26.2 %reduce-scatter.5.cloned.1.call-done = bf16[256,1536]{1,0:T(8,128)(2,1)} async-done(((bf16[512,1536]{1,0:T(8,128)(2,1)}), bf16[256,1536]{1,0:T(8,128)(2,1)}) %reduce-scatter.5.cloned.1.call-update) | async-done | bytes 786448 | tf_op jit(solution)/shard_map/reduce_scatter | solution.py:79
  83.6 1.5 multiply_reduce_fusion.1
  87.5 26.3 %all-gather.7.cloned.1.call-done = bf16[512,1536]{1,0:T(8,128)(2,1)} async-done(((bf16[256,1536]{1,0:T(8,128)(2,1)}), bf16[512,1536]{1,0:T(8,128)(2,1)}) %all-gather.7.cloned.1.call-update) | async-done | bytes 1572880 | tf_op jit(solution)/shard_map/all_gather | solution.py:154
  113.8 8.8 %fusion.52 = f32[512,2048]{1,0:T(8,128)} fusion(bf16[512,1536]{1,0:T(8,128)(2,1)} %all-gather.7.cloned.1.call-done, bf16[1536,2048]{1,0:T(8,128)(2,1)} %param.20), kind=kOutput, calls=%fused_computation.122 | convolution fusion | flops 3221225472 | bytes 12058624 | tf_op jit(solution)/shard_map/dot_general | solution.py:16
  122.6 8.2 %fusion.53 = f32[512,2048]{1,0:T(8,128)} fusion(bf16[512,1536]{1,0:T(8,128)(2,1)S(1)} %copy-done.47, bf16[1536,2048]{1,0:T(8,128)(2,1)} %param.21), kind=kOutput, calls=%fused_computation.123 | convolution fusion | flops 3221225472 | bytes 12058624 | tf_op jit(solution)/shard_map/dot_general | solution.py:16
  130.8 11.7 %all-gather.9.cloned.1.call-done = bf16[512,1536]{1,0:T(8,128)(2,1)} async-done(((bf16[256,1536]{1,0:T(8,128)(2,1)}), bf16[512,1536]{1,0:T(8,128)(2,1)}) %all-gather.9.cloned.1.call-update) | async-done | bytes 1572880 | tf_op jit(solution)/shard_map/all_gather | solution.py:168
  142.5 11.7 %multiply_convert_fusion = (bf16[512,2048]{1,0:T(8,128)(2,1)S(1)}, bf16[512,2048]{1,0:T(8,128)(2,1)S(1)}, bf16[512,2048]{1,0:T(8,128)(2,1)}) fusion(f32[512,2048]{1,0:T(8,128)} %fusion.52, f32[512,2048]{1,0:T(8,128)} %fusion.53, bf16[512,1536]{1,0:T(8,128)(2,1)} %all-gather.9.cloned.1.call-done, bf16[2048,1536]{1,0:T(8,128)(2,1)} %param.22), kind=kOutput, calls=%fused_computation.17 | convolution fusion | flops 3238002688 | bytes 22544384 | tf_op jit(solution)/shard_map/dot_general | solution.py:26
  154.2 7.3 fusion.54
  161.5 7.6 fusion.12
  169.4 8.0 convolution_convert_fusion.5
  177.4 18.0 %reduce-scatter.9.cloned.1.call-done = bf16[256,1536]{1,0:T(8,128)(2,1)} async-done(((bf16[512,1536]{1,0:T(8,128)(2,1)}), bf16[256,1536]{1,0:T(8,128)(2,1)}) %reduce-scatter.9.cloned.1.call-update) | async-done | bytes 786448 | tf_op jit(solution)/shard_map/reduce_scatter | solution.py:79
  195.4 28.8 %reduce-scatter.7.cloned.1.call-done = bf16[256,1536]{1,0:T(8,128)(2,1)} async-done(((bf16[512,1536]{1,0:T(8,128)(2,1)}), bf16[256,1536]{1,0:T(8,128)(2,1)}) %reduce-scatter.7.cloned.1.call-update) | async-done | bytes 786448 | tf_op jit(solution)/shard_map/reduce_scatter | solution.py:79
  224.2 4.4 fusion.28
  228.6 1.6 fusion.48
  231.0 26.6 %all-gather.11.cloned.1.call-done = bf16[512,1536]{1,0:T(8,128)(2,1)} async-done(((bf16[256,1536]{1,0:T(8,128)(2,1)}), bf16[512,1536]{1,0:T(8,128)(2,1)}) %all-gather.11.cloned.1.call-update) | async-done | bytes 1572880 | tf_op jit(solution)/shard_map/all_gather | solution.py:182
  257.6 3.7 convolution_convert_fusion.9
  262.7 5.1 fusion.39
  267.8 5.2 fusion
  273.1 2.6 fusion.2
  278.5 1.6 copy-done.44
  280.1 1.4 fusion.55
  282.9 2.2 fusion.11
  285.4 7.1 convolution_convert_fusion.1
  292.5 5.3 convolution_convert_fusion.2
  297.9 5.4 convolution_convert_fusion
  303.3 2.0 convolution_convert_fusion.7
  305.3 2.0 convolution_convert_fusion.8
  307.4 2.8 convolution_convert_fusion.4
  310.2 2.8 convolution_convert_fusion.3
  313.1 2.1 pad_maximum_fusion.4
  315.2 1.6 fusion.32
  316.9 41.7 %all-reduce = (f32[2,1536]{1,0:T(2,128)S(1)}, f32[3]{0:T(128)S(1)}) all-reduce(f32[2,1536]{1,0:T(2,128)S(1)} %pad_maximum_fusion.3, f32[3]{0:T(128)S(1)} %pad_maximum_fusion.4), channel_id=1, replica_groups=mesh['dp'=16,'tensor'=2] {'dp','tensor'}, use_global_device_ids=true, to_apply=%region_16.17 | all-reduce | flops 3075 | bytes 24600 | tf_op jit(solution)/shard_map/psum | solution.py:241
  359.7 3.4 fusion.21
  363.1 413.0 %all-reduce.4.cloned.1.call-done = (bf16[1536,768]{1,0:T(8,128)(2,1)}, bf16[1536,384]{1,0:T(8,128)(2,1)}, bf16[1536,384]{1,0:T(8,128)(2,1)}, bf16[768,1536]{1,0:...) async-done(((bf16[1536,768]{1,0:T(8,128)(2,1)}, bf16[1536,384]{1,0:T(8,128)(2,1)}, bf16[1536,384]{1,0:T(8,128)(2,1)}, ...) | async-done | bytes 25952272 | tf_op jit(solution)/shard_map/psum | solution.py:74
  776.1 9.2 %convert_element_type.196 = f32[1536,2048]{1,0:T(8,128)} convert(bf16[1536,2048]{1,0:T(8,128)(2,1)} %get-tuple-element.95) | non-fusion elementwise | flops 3145728 | bytes 18874368 | tf_op jit(solution)/shard_map/convert_element_type | solution.py:75
  785.3 6.3 convert_element_type.198
  791.6 6.6 convert_element_type.200
  798.2 2.5 convert_element_type.188
  800.8 2.8 convert_element_type.194
  803.6 1.6 convert_element_type.190
  805.3 1.6 convert_element_type.192
  (173 shorter events, 18.8 us)
Async XLA Ops:
  7.2 47.6 %copy-start = (bf16[768,1536]{1,0:T(8,128)(2,1)S(1)}, bf16[768,1536]{1,0:T(8,128)(2,1)}, u32[]{:S(2)}) copy-start(bf16[768,1536]{1,0:T(8,128)(2,1)} %param.18) | copy-start | bytes 7077892
  7.2 4.0 copy-start.51
  7.2 33.9 %all-gather.5.cloned.1.call-start = ((), (), s32[]{:S(2)}) async-start(), calls=%async_computation.4 | async-start | bytes 2359296 | tf_op jit(solution)/shard_map/all_gather | solution.py:101
  11.1 72.5 %reduce-scatter.5.cloned.1.call-start = ((), (), s32[]{:S(2)}) async-start(), calls=%async_computation.5 | async-start | bytes 2359296 | tf_op jit(solution)/shard_map/reduce_scatter | solution.py:79
  41.1 4.0 copy-start.45
  48.9 3.4 copy-start.2
  51.0 2.9 copy-start.37
  54.8 28.8 %copy-start.3 = (bf16[256,1536]{1,0:T(8,128)(2,1)S(1)}, bf16[256,1536]{1,0:T(8,128)(2,1)}, u32[]{:S(2)}) copy-start(bf16[256,1536]{1,0:T(8,128)(2,1)} %param.12) | copy-start | bytes 2359300
  57.4 27.8 %copy-start.35 = (f32[1536]{0:T(1024)S(1)}, f32[1536]{0:T(1024)}, u32[]{:S(2)}) copy-start(f32[1536]{0:T(1024)} %param.19) | copy-start | bytes 18436
  57.4 56.4 %all-gather.7.cloned.1.call-start = ((), (), s32[]{:S(2)}) async-start(), calls=%async_computation.6 | async-start | bytes 2359296 | tf_op jit(solution)/shard_map/all_gather | solution.py:154
  85.2 143.4 %copy-start.38 = (f32[256]{0:T(256)}, f32[256]{0:T(256)S(1)}, u32[]{:S(2)}) copy-start(f32[256]{0:T(256)S(1)} %add_rsqrt_fusion) | copy-start | bytes 3076
  86.4 56.1 %all-gather.9.cloned.1.call-start = ((), (), s32[]{:S(2)}) async-start(), calls=%async_computation.8 | async-start | bytes 2359296 | tf_op jit(solution)/shard_map/all_gather | solution.py:168
  87.0 108.4 %reduce-scatter.9.cloned.1.call-start = ((), (), s32[]{:S(2)}) async-start(), calls=%async_computation.9 | async-start | bytes 2359296 | tf_op jit(solution)/shard_map/reduce_scatter | solution.py:79
  113.8 8.8 %copy-start.47 = (bf16[512,1536]{1,0:T(8,128)(2,1)S(1)}, bf16[512,1536]{1,0:T(8,128)(2,1)}, u32[]{:S(2)}) copy-start(bf16[512,1536]{1,0:T(8,128)(2,1)} %all-gather.7.cloned.1.call-done) | copy-start | bytes 4718596
  154.2 7.3 copy-start.52
  154.2 7.3 copy-start.54
  169.1 55.0 %reduce-scatter.7.cloned.1.call-start = ((), (), s32[]{:S(2)}) async-start(), calls=%async_computation.7 | async-start | bytes 2359296 | tf_op jit(solution)/shard_map/reduce_scatter | solution.py:79
  177.4 80.2 %all-gather.11.cloned.1.call-start = ((), (), s32[]{:S(2)}) async-start(), calls=%async_computation.10 | async-start | bytes 2359296 | tf_op jit(solution)/shard_map/all_gather | solution.py:182
  224.2 4.4 copy-start.5
  224.2 4.4 copy-start.9
  224.2 4.4 copy-start.11
  230.3 85.0 %reduce-scatter.11.cloned.1.call-start = ((), (), s32[]{:S(2)}) async-start(), calls=%async_computation.11 | async-start | bytes 2359296 | tf_op jit(solution)/shard_map/reduce_scatter | solution.py:79
  262.7 5.1 copy-start.27
  262.7 10.3 %slice-start = ((s8[8388608]{0:T(1024)(128)(4,1)}), s8[4194304]{0:T(1024)(128)(4,1)S(1)}, s32[]{:S(2)}) async-start(s8[8388608]{0:T(1024)(128)(4,1)} %bitcast.116), calls=%async_computation.13 | async-start | bytes 8388608
  267.8 14.9 %copy-start.33 = (bf16[4,96,512]{2,1,0:T(8,128)(2,1)}, bf16[4,96,512]{2,1,0:T(8,128)(2,1)S(1)}, u32[]{:S(2)}) copy-start(bf16[4,96,512]{2,1,0:T(8,128)(2,1)S(1)} %fusion.39) | copy-start | bytes 1179652
  267.8 5.2 slice-start.1
  273.1 2.6 copy-start.8
  278.5 3.1 copy-start.31
  285.1 491.0 %all-reduce.4.cloned.1.call-start = ((), (), s32[]{:S(2)}) async-start(), calls=%async_computation.12 | async-start | bytes 51904512 | tf_op jit(solution)/shard_map/psum | solution.py:74
  285.4 7.1 copy-start.53
  292.5 5.4 copy-start.49
  292.5 5.4 copy-start.55
  297.9 5.4 copy-start.34
  297.9 5.4 copy-start.46
  307.4 2.9 copy-start.30
  307.4 2.9 copy-start.50
  313.0 46.7 %copy-start.12 = (bf16[256,1536]{1,0:T(8,128)(2,1)S(1)}, bf16[256,1536]{1,0:T(8,128)(2,1)}, u32[]{:S(2)}) copy-start(bf16[256,1536]{1,0:T(8,128)(2,1)} %reduce-scatter.9.cloned.1.call-done) | copy-start | bytes 2359300
  313.0 46.7 %copy-start.39 = (f32[256]{0:T(256)S(1)}, f32[256]{0:T(256)}, u32[]{:S(2)}) copy-start(f32[256]{0:T(256)} %copy-done.38) | copy-start | bytes 3076
  313.0 46.7 %copy-start.43 = (f32[256]{0:T(256)S(1)}, f32[256]{0:T(256)}, u32[]{:S(2)}) copy-start(f32[256]{0:T(256)} %copy-done.42) | copy-start | bytes 3076
  313.1 46.6 %copy-start.6 = (bf16[256,1536]{1,0:T(8,128)(2,1)S(1)}, bf16[256,1536]{1,0:T(8,128)(2,1)}, u32[]{:S(2)}) copy-start(bf16[256,1536]{1,0:T(8,128)(2,1)} %reduce-scatter.5.cloned.1.call-done) | copy-start | bytes 2359300
  313.1 46.6 %copy-start.10 = (bf16[256,1536]{1,0:T(8,128)(2,1)S(1)}, bf16[256,1536]{1,0:T(8,128)(2,1)}, u32[]{:S(2)}) copy-start(bf16[256,1536]{1,0:T(8,128)(2,1)} %param.23) | copy-start | bytes 2359300
  776.1 9.3 %copy-start.13 = (bf16[1536,2048]{1,0:T(8,128)(2,1)S(1)}, bf16[1536,2048]{1,0:T(8,128)(2,1)}, u32[]{:S(2)}) copy-start(bf16[1536,2048]{1,0:T(8,128)(2,1)} %get-tuple-element.96) | copy-start | bytes 18874372
  776.1 15.5 %slice-start.2 = ((s8[6291456]{0:T(1024)(128)(4,1)}), s8[4194304]{0:T(1024)(128)(4,1)S(1)}, s32[]{:S(2)}) async-start(s8[6291456]{0:T(1024)(128)(4,1)} %bitcast.121), calls=%async_computation.15 | async-start | bytes 8388608
  785.3 6.3 slice-start.3
  791.6 6.6 copy-start.15
  798.2 2.5 copy-start.14
  800.8 2.8 copy-start.21
  803.6 3.3 copy-start.1
  (21 other events, 36.3 us)
Sparse Core Ops, SparseCore 0:
  11.2 29.8 all-gather.4
  57.5 26.0 reduce-scatter.4
  86.5 27.2 all-gather.6
  115.3 27.2 all-gather.8
  169.3 26.0 reduce-scatter.8
  198.1 26.0 reduce-scatter.6
  230.4 27.2 all-gather.10
  285.3 26.0 reduce-scatter.10
  318.3 457.7 all-reduce.3

commit v2 on v1

--- a/solution.py
+++ b/solution.py
@@ -1,6 +1,10 @@
+from functools import partial
+
 import jax
 import jax.numpy as jnp
 from jax import lax
+from jax.experimental import pallas as pl
+from jax.experimental.pallas import tpu as pltpu
 from jax.sharding import PartitionSpec as P
 
 HD = 96
@@ -70,6 +74,437 @@
     return (gain_rows, inv_rms * (scaled - values * inv_rms * inv_rms * row_inner))
 
 
+ORDER = (
+    0, 1, 5, 10, 11, 2, 6, 4, 11, 7, 3, 9, 14, 11, 8, 13, 10, 11, 11, 13, 13, 14, 11, 10, 13, 13,
+    11, 10, 13, 12, 13, 14, 18, 10, 14, 11, 13, 12, 14, 10, 11, 12, 13, 18, 19, 10, 14, 11, 11, 17,
+    12, 18, 16, 13, 13, 10, 10, 16, 19, 14, 18, 12, 19, 15, 14, 14, 17, 18, 16, 10, 17, 19, 19, 12,
+    16, 17, 17, 15, 12, 14, 16, 19, 17, 19, 12, 12, 17, 15, 18, 16, 19, 15, 15, 17, 18, 12, 16, 15,
+    19, 17, 18, 18, 15, 16, 16, 19, 19, 17, 17, 15, 18, 15, 16, 15, 15,
+)
+
+
+MESH = pl.DeviceIdType.MESH
+LINE = 4
+UNITS = (
+    (2048, 1536, 640, 384, 256),
+    (1536, 2048, 512, 256, 256),
+    (1536, 2048, 384, 384, 256),
+    (768, 1536, 256, 128, 128),
+    (1536, 1536, 512, 256, 256),
+)
+COPIES = 16
+TILE_BASE = 2 * len(UNITS) * COPIES
+TILES = tuple(rows // 2 // tile for rows, _, _, _, tile in UNITS)
+SMALL_BASE = TILE_BASE + sum(TILES)
+SMALL_STEPS = 5
+N_SEMS = SMALL_BASE + SMALL_STEPS
+
+
+def rows_at(start, size):
+    return pl.ds(pl.multiple_of(start, 16), size)
+
+
+class Place:
+    def __init__(self):
+        dp = lax.axis_index("dp")
+        self.dp = dp
+        self.y = lax.axis_index("tensor")
+        self.core = lax.rem(dp, 2)
+        self.x = lax.rem(dp // 2, 2)
+        self.z = dp // 4
+
+    def at(self, z, x, core, y):
+        return ((z * 2 + x) * 2 + core, y)
+
+    def other_core(self):
+        return self.at(self.z, self.x, 1 - self.core, self.y)
+
+    def other_x(self):
+        return self.at(self.z, 1 - self.x, self.core, self.y)
+
+    def other_y(self):
+        return self.at(self.z, self.x, self.core, 1 - self.y)
+
+    def up(self):
+        return self.at(self.z + 1, self.x, self.core, self.y)
+
+    def down(self):
+        return self.at(self.z - 1, self.x, self.core, self.y)
+
+    def pair_z(self):
+        return self.at(self.z + 1 - 2 * lax.rem(self.z, 2), self.x, self.core, self.y)
+
+    def far_z(self):
+        return self.at(lax.rem(self.z + 2, LINE), self.x, self.core, self.y)
+
+
+class Mover:
+    def __init__(self, send_sems, recv_sems):
+        self.send_sems = send_sems
+        self.recv_sems = recv_sems
+        self.left = []
+
+    def copy(self, source, target, index, device):
+        return pltpu.make_async_remote_copy(
+            src_ref=source,
+            dst_ref=target,
+            send_sem=self.send_sems.at[index],
+            recv_sem=self.recv_sems.at[index],
+            device_id=device,
+            device_id_type=MESH,
+        )
+
+    def start(self, source, target, index, device, when=None):
+        copy = self.copy(source, target, index, device)
+        guarded(when, copy.start)
+        self.left.append((when, copy.wait_send))
+
+    def arrived(self, target, index, device):
+        self.copy(target, target, index, device).wait_recv()
+
+
+def guarded(when, action):
+    if when is None:
+        action()
+    else:
+        pl.when(when)(action)
+
+
+def add_rows(target, target_row, source, source_row, size):
+    step = 16
+
+    def one(i, _):
+        here = rows_at(target_row + i * step, step)
+        there = rows_at(source_row + i * step, step)
+        total = target[here, :].astype(jnp.float32) + source[there, :].astype(jnp.float32)
+        target[here, :] = total.astype(target.dtype)
+        return 0
+
+    lax.fori_loop(0, size // step, one, 0)
+
+
+class Block:
+    def __init__(self, place, mover, held, across, along, result, base, start, size, half_rows, x_first):
+        self.p = place
+        self.m = mover
+        self.held = held
+        self.across = across
+        self.along = along
+        self.result = result
+        self.base = base
+        self.start = start
+        self.size = size
+        self.half_rows = half_rows
+        self.x_first = x_first
+        self.chunk = size // 8 if x_first else size // 4
+        self.origin = start + place.x * (size // 2) if x_first else start
+
+    def part(self, chunk):
+        return self.held.at[rows_at(self.origin + chunk * self.chunk, self.chunk)]
+
+    def final(self, row, size):
+        return self.result.at[rows_at(self.p.core * self.half_rows + row, size)]
+
+    def final_part(self, chunk):
+        return self.final(self.origin + chunk * self.chunk, self.chunk)
+
+    def keep(self, row, size):
+        index = self.base // COPIES
+        copy = pltpu.make_async_copy(
+            self.held.at[rows_at(row, size)], self.final(row, size), self.m.keep_sems.at[index]
+        )
+        copy.start()
+        self.kept = copy
+
+    def events(self):
+        line = [self.line_start, lambda: self.line_add(0), lambda: self.line_add(1), lambda: self.line_add(2)]
+        spread = [lambda: self.spread(1), lambda: self.spread(2), lambda: self.spread(3)]
+        if self.x_first:
+            return [self.x_send, self.x_add] + line[1:] + spread + [self.x_return, self.x_done]
+        return line + [self.pair_send, self.pair_add, self.pair_done] + spread + [self.z_done]
+
+    def line_start(self):
+        p = self.p
+        for step in range(3):
+            self.m.start(self.part(3 - step), self.along.at[step], self.base + step, p.up(), p.z == 0)
+            self.m.start(self.part(step), self.along.at[3 + step], self.base + 3 + step, p.down(), p.z == LINE - 1)
+
+    def line_add(self, step):
+        p = self.p
+        rising = jnp.minimum(p.z + 2 - step, 3)
+        falling = jnp.maximum(p.z - 2 + step, 0)
+        goes_up = (p.z >= 1) & (p.z <= step + 1)
+        goes_down = (p.z <= 2) & (p.z >= 2 - step)
+
+        def take_rising():
+            self.m.arrived(self.along.at[step], self.base + step, p.down())
+            add_rows(self.held, self.origin + rising * self.chunk, self.along.at[step], 0, self.chunk)
+
+        def take_falling():
+            self.m.arrived(self.along.at[3 + step], self.base + 3 + step, p.up())
+            add_rows(self.held, self.origin + falling * self.chunk, self.along.at[3 + step], 0, self.chunk)
+
+        pl.when(goes_up)(take_rising)
+        if step < 2:
+            self.m.start(self.part(rising), self.along.at[step + 1], self.base + step + 1, p.up(), goes_up)
+        pl.when(goes_down)(take_falling)
+        if step < 2:
+            self.m.start(self.part(falling), self.along.at[4 + step], self.base + 4 + step, p.down(), goes_down)
+        elif self.x_first:
+            self.keep(self.origin + p.z * self.chunk, self.chunk)
+            self.own_spread(self.part(p.z))
+
+    def own_spread(self, source):
+        p = self.p
+        target = self.final_part(p.z)
+        self.m.start(source, target, self.base + 6, p.up(), p.z < 3)
+        self.m.start(source, target, self.base + 9, p.down(), p.z > 0)
+
+    def spread(self, distance):
+        p = self.p
+        below = self.final_part(jnp.maximum(p.z - distance, 0))
+        above = self.final_part(jnp.minimum(p.z + distance, 3))
+
+        pl.when(p.z >= distance)(lambda: self.m.arrived(below, self.base + 5 + distance, p.down()))
+        if distance < 3:
+            self.m.start(below, below, self.base + 6 + distance, p.up(), (p.z >= distance) & (p.z < 3))
+        pl.when(p.z <= 3 - distance)(lambda: self.m.arrived(above, self.base + 8 + distance, p.up()))
+        if distance < 3:
+            self.m.start(above, above, self.base + 9 + distance, p.down(), (p.z <= 3 - distance) & (p.z > 0))
+
+    def x_part(self, which):
+        half = self.size // 2
+        return self.held.at[rows_at(self.start + which * half, half)]
+
+    def x_send(self):
+        self.m.start(self.x_part(1 - self.p.x), self.across, self.base + 12, self.p.other_x())
+
+    def x_add(self):
+        self.m.arrived(self.across, self.base + 12, self.p.other_x())
+        add_rows(self.held, self.origin, self.across, 0, self.size // 2)
+        self.line_start()
+
+    def x_final(self, which):
+        half = self.size // 2
+        return self.final(self.start + which * half, half)
+
+    def x_return(self):
+        p = self.p
+        self.kept.wait()
+        mine = self.x_final(p.x)
+        self.m.start(mine, mine, self.base + 13, p.other_x())
+        self.give(p.x * (self.size // 2), self.size // 2, 14)
+
+    def x_done(self):
+        p = self.p
+        self.m.arrived(self.x_final(1 - p.x), self.base + 13, p.other_x())
+        self.give((1 - p.x) * (self.size // 2), self.size // 2, 15)
+
+    def pair_row(self, which):
+        return self.start + self.p.z * self.chunk + which * (self.chunk // 2)
+
+    def pair_send(self):
+        half = self.chunk // 2
+        source = self.held.at[rows_at(self.pair_row(1 - self.p.x), half)]
+        self.m.start(source, self.across, self.base + 12, self.p.other_x())
+
+    def pair_add(self):
+        p = self.p
+        half = self.chunk // 2
+        self.m.arrived(self.across, self.base + 12, p.other_x())
+        row = self.pair_row(p.x)
+        add_rows(self.held, row, self.across, 0, half)
+        self.keep(row, half)
+        self.m.start(self.held.at[rows_at(row, half)], self.final(row, half), self.base + 13, p.other_x())
+
+    def pair_done(self):
+        p = self.p
+        half = self.chunk // 2
+        self.m.arrived(self.final(self.pair_row(1 - p.x), half), self.base + 13, p.other_x())
+        self.kept.wait()
+        self.own_spread(self.final_part(p.z))
+
+    def z_done(self):
+        self.give(0, self.size, 14)
+
+    def give(self, offset, size, slot):
+        p = self.p
+        source = self.final(self.start + offset, size)
+        self.m.start(source, source, self.base + slot, p.other_core())
+        other = self.result.at[rows_at((1 - p.core) * self.half_rows + self.start + offset, size)]
+        self.m.left.append((None, lambda: self.m.arrived(other, self.base + slot, p.other_core())))
+
+
+def product_tile(left, right, first, tile, width, part):
+    columns = pl.ds(pl.multiple_of(first, 128), tile)
+    return lax.dot_general(
+        left[:, columns], right[:, part * width : (part + 1) * width],
+        (((0,), (0,)), ((), ())), preferred_element_type=jnp.float32,
+    )
+
+
+class Unit:
+    def __init__(self, index, place, mover, left, right, held, staged, stage_sems):
+        self.index = index
+        self.rows, self.columns, _, _, self.tile = UNITS[index]
+        self.p, self.m = place, mover
+        self.left, self.right, self.held = left, right, held
+        self.staged, self.stage_sems = staged, stage_sems
+        self.base = TILE_BASE + sum(TILES[:index])
+        self.width = 512
+
+    def tile_copy(self, i, slot):
+        tile = self.tile
+        return pltpu.make_async_remote_copy(
+            src_ref=self.staged.at[slot, pl.ds(0, tile), pl.ds(0, self.columns)],
+            dst_ref=self.held.at[rows_at(i * tile, tile)],
+            send_sem=self.stage_sems.at[slot],
+            recv_sem=self.m.recv_sems.at[self.base + i],
+            device_id=self.p.other_core(),
+            device_id_type=MESH,
+        )
+
+    def send(self):
+        half, tile = self.rows // 2, self.tile
+
+        def one(i, _):
+            slot = lax.rem(i, 2)
+            pl.when(i >= 2)(lambda: self.tile_copy(i, slot).wait_send())
+            first = (1 - self.p.core) * half + i * tile
+            for part in range(self.columns // self.width):
+                got = product_tile(self.left, self.right, first, tile, self.width, part)
+                self.staged[slot, pl.ds(0, tile), part * self.width : (part + 1) * self.width] = got.astype(
+                    jnp.bfloat16
+                )
+            self.tile_copy(i, slot).start()
+            return 0
+
+        lax.fori_loop(0, half // tile, one, 0)
+        for slot in range(min(2, half // tile)):
+            self.tile_copy(0, slot).wait_send()
+
+    def own(self):
+        half, tile = self.rows // 2, self.tile
+
+        def one(i, _):
+            self.tile_copy(i, 0).wait_recv()
+            first = self.p.core * half + i * tile
+            here = rows_at(i * tile, tile)
+            for part in range(self.columns // self.width):
+                got = product_tile(self.left, self.right, first, tile, self.width, part)
+                cut = slice(part * self.width, (part + 1) * self.width)
+                total = got + self.held[here, cut].astype(jnp.float32)
+                self.held[here, cut] = total.astype(jnp.bfloat16)
+            return 0
+
+        lax.fori_loop(0, half // tile, one, 0)
+
+
+def sum_small(place, mover, total, slots, step):
+    device = (place.other_core, place.other_x, place.other_y, place.pair_z, place.far_z)[step]()
+    index = SMALL_BASE + step
+    copy = mover.copy(total.at[step], slots.at[step], index, device)
+    copy.start()
+    copy.wait()
+    total[step + 1] = total[step] + slots[step]
+
+
+def grads_kernel(
+    hid, g, h2, d_gate, d_up, o, d_attn, h1, d_qkv, small,
+    down_out, gate_out, up_out, o_out, qkv_out, small_out,
+    held0, held1, held2, held3, held4, staged,
+    ax0, az0, ax1, az1, ax2, az2, ax3, az3, ax4, az4,
+    lx0, lz0, lx1, lz1, lx2, lz2, lx3, lz3, lx4, lz4,
+    totals, slots, stage_sems, send_sems, recv_sems, keep_sems,
+):
+    place = Place()
+    mover = Mover(send_sems, recv_sems)
+    mover.keep_sems = keep_sems
+    enter(place)
+    held = (held0, held1, held2, held3, held4)
+    across = (ax0, az0, ax1, az1, ax2, az2, ax3, az3, ax4, az4)
+    along = (lx0, lz0, lx1, lz1, lx2, lz2, lx3, lz3, lx4, lz4)
+    lefts = (hid, h2, h2, o, h1)
+    rights = (g, d_gate, d_up, d_attn, d_qkv)
+    results = (down_out, gate_out, up_out, o_out, qkv_out)
+    units = [
+        Unit(i, place, mover, lefts[i], rights[i], held[i], staged, stage_sems) for i in range(len(UNITS))
+    ]
+    steps = []
+    for i, (rows, columns, x_rows, z_rows, _) in enumerate(UNITS):
+        for j in range(2):
+            b = 2 * i + j
+            block = Block(
+                place, mover, held[i], across[b], along[b], results[i], b * COPIES,
+                0 if j == 0 else x_rows, x_rows if j == 0 else z_rows, rows // 2, j == 0,
+            )
+            steps.append(block.events())
+    totals[0] = small[...]
+    small_at = 0
+    for count, item in enumerate(ORDER):
+        if item < 5:
+            units[item].send()
+        elif item < 10:
+            units[item - 5].own()
+        else:
+            steps[item - 10].pop(0)()
+        if count % 8 == 7 and small_at < SMALL_STEPS:
+            sum_small(place, mover, totals, slots, small_at)
+            small_at += 1
+    small_out[...] = totals[SMALL_STEPS]
+    for when, wait in mover.left:
+        guarded(when, wait)
+
+
+def enter(place):
+    barrier = pltpu.get_barrier_semaphore()
+
+    def greet(device):
+        pl.semaphore_signal(barrier, inc=1, device_id=device, device_id_type=MESH)
+
+    for device in (place.other_core(), place.other_x(), place.other_y(), place.pair_z(), place.far_z()):
+        greet(device)
+    middle = (place.z == 1) | (place.z == 2)
+    pl.when(middle)(lambda: greet(place.at(3 - place.z, place.x, place.core, place.y)))
+    pl.semaphore_wait(barrier, 5 + jnp.where(middle, 1, 0))
+
+
+def weight_grads(hid, g, h2, d_gate, d_up, o, d_attn, h1, d_qkv, small):
+    vmem = pl.BlockSpec(memory_space=pltpu.VMEM)
+    hbm = pl.BlockSpec(memory_space=pl.ANY)
+    low = jnp.bfloat16
+    held = [pltpu.VMEM((rows // 2, columns), low) for rows, columns, *_ in UNITS]
+    across, along = [], []
+    for _, columns, x_rows, z_rows, _ in UNITS:
+        across += [pltpu.VMEM((x_rows // 2, columns), low), pltpu.VMEM((z_rows // 8, columns), low)]
+        along += [pltpu.VMEM((6, x_rows // 8, columns), low), pltpu.VMEM((6, z_rows // 4, columns), low)]
+    flops = sum(2 * 512 * rows * columns for rows, columns, *_ in UNITS)
+    return pl.pallas_call(
+        grads_kernel,
+        out_shape=[jax.ShapeDtypeStruct((rows, columns), low) for rows, columns, *_ in UNITS]
+        + [jax.ShapeDtypeStruct(small.shape, jnp.float32)],
+        in_specs=[vmem] * 10,
+        out_specs=[hbm] * 5 + [vmem],
+        scratch_shapes=held
+        + [pltpu.VMEM((2, 256, 2048), low)]
+        + across
+        + along
+        + [
+            pltpu.VMEM((SMALL_STEPS + 1,) + small.shape, jnp.float32),
+            pltpu.VMEM((SMALL_STEPS,) + small.shape, jnp.float32),
+            pltpu.SemaphoreType.DMA((2,)),
+            pltpu.SemaphoreType.DMA((N_SEMS,)),
+            pltpu.SemaphoreType.DMA((N_SEMS,)),
+            pltpu.SemaphoreType.DMA((2 * len(UNITS),)),
+        ],
+        compiler_params=pltpu.CompilerParams(
+            collective_id=0, has_side_effects=True, vmem_limit_bytes=60 << 20
+        ),
+        cost_estimate=pl.CostEstimate(flops=flops, bytes_accessed=80 << 20, transcendentals=0),
+        name="weight_grads",
+    )(hid, g, h2, d_gate, d_up, o, d_attn, h1, d_qkv, small)
+
+
 def dp_sum(terms):
     low = lax.psum(tuple(term.astype(jnp.bfloat16) for term in terms), "dp")
     return tuple(term.astype(jnp.float32) for term in low)
@@ -82,6 +517,7 @@
 
 
 def body(
+    fused,
     tokens,
     lengths,
     first_gain,
@@ -173,7 +609,8 @@
     grad_up = (grad_hidden * gate_value * gate_sig).astype(jnp.bfloat16)
     gate_g = times_rows(full_second, grad_gate)
     up_g = times_rows(full_second, grad_up)
-    gate_g, up_g, down_g = dp_sum((gate_g, up_g, down_g))
+    if not fused:
+        gate_g, up_g, down_g = dp_sum((gate_g, up_g, down_g))
     grad_normed2 = low_scatter(
         times_cols(grad_gate, gate_weight) + times_cols(grad_up, up_weight)
     )
@@ -237,8 +674,24 @@
     first_rows, grad_in_norm = norm_back(inputs, inv_first, first_gain, grad_normed1)
     tokens_grad = grad_middle + grad_in_norm
     gain_rows = jnp.stack([first_rows, second_rows])
-    query_g, key_g, value_g, output_g = dp_sum((query_g, key_g, value_g, output_g))
-    gain_rows, squares = lax.psum((gain_rows, squares), ("dp", "tensor"))
+    if fused:
+        small = jnp.concatenate(
+            [gain_rows, jnp.pad(squares, (0, gain_rows.shape[1] - 3))[None]], axis=0
+        )
+        small = jnp.pad(small, ((0, 5), (0, 0)))
+        *sums, small = weight_grads(
+            hidden, grad_full, full_second, grad_gate, grad_up, attended, grad_attn_full, full_first,
+            jnp.concatenate([query_lin, key_lin, value_lin], axis=1), small,
+        )
+        down_g, gate_g, up_g, output_g, qkv_g = (part.astype(jnp.float32) for part in sums)
+        q_cols, k_cols = query_lin.shape[1], key_lin.shape[1]
+        query_g = qkv_g[:, :q_cols]
+        key_g = qkv_g[:, q_cols : q_cols + k_cols]
+        value_g = qkv_g[:, q_cols + k_cols :]
+        gain_rows, squares = small[:2], small[2, :3]
+    else:
+        query_g, key_g, value_g, output_g = dp_sum((query_g, key_g, value_g, output_g))
+        gain_rows, squares = lax.psum((gain_rows, squares), ("dp", "tensor"))
     rms_values = jnp.sqrt(squares / (total_rows * lax.axis_size("dp")))
     return (
         layer_out.astype(jnp.bfloat16),
@@ -285,4 +738,5 @@
         P("tensor", None),
         P(),
     )
-    return jax.shard_map(body, mesh=mesh, in_specs=in_specs, out_specs=out_specs, check_vma=False)
+    fused = dict(mesh.shape) == {"dp": 16, "tensor": 2}
+    return jax.shard_map(partial(body, fused), mesh=mesh, in_specs=in_specs, out_specs=out_specs, check_vma=False)

time: 822 us -> 649 us (0.79)
  waiting for transfers between devices: 580 us -> 178 us
  Pallas kernels: 0 us -> 283 us
  blocking collectives: 41.7 us -> 0 us
  matrix products: 111 us -> 83.5 us
  local copies, waits for them, and re-layouts: 7.52 us -> 18.6 us
    psum x1 -> x0, waiting for transfers between devices: 413 us -> none  [dp_sum(): low = lax.psum(tuple((term.astype(jnp.bfloat16) for term in terms)), 'dp')]
    pallas_call x0 -> x1, Pallas kernels: none -> 283 us  [weight_grads(): pl.pallas_call(grads_kernel, out_shape=[jax.ShapeDtypeStruct((rows, colum...]
    psum x1 -> x0, blocking collectives: 41.7 us -> none  [body(): gain_rows, squares = lax.psum((gain_rows, squares), ('dp', 'tensor'))]
    dot_general x7 -> x0, matrix products: 27.5 us -> none  [times_rows(): lax.dot_general(left_side, right_side, (((0,), (0,)), ((), ())), preferre...]
    reduce_scatter x4, waiting for transfers between devices: 72.9 us -> 93.1 us  [low_scatter(): lax.psum_scatter(partial.astype(jnp.bfloat16), 'tensor', scatter_dimensio...]
    all_gather x1, waiting for transfers between devices: 26.6 us -> 18.1 us  [body(): lax.all_gather(grad_middle.astype(jnp.bfloat16), 'tensor', axis=0, tiled=...]
    convert_element_type x7 -> x4, other arithmetic: 30.6 us -> 24.9 us  [body(): part.astype(jnp.float32)]
  transfers between devices with their start and end apart: 9 -> 8, of which waited for: 8 -> 8; matrix products, arithmetic and copies ran while one was open for 8% -> 5% of each run, Pallas kernels for 0% -> 0%
where the time goes in v2:
time: 649 us; the launch traced here: 641 us
  Pallas kernels  283 us (44%)
  waiting for transfers between devices  178 us (27%)
  matrix products  83.5 us (13%)
  other arithmetic  53.6 us (8%)
  local copies, waits for them, and re-layouts  18.6 us (3%)
  between operations  15.3 us (2%)
  starting transfers between devices  9.06 us (1%)
    pallas_call x1, Pallas kernels, weight_grads(): pl.pallas_call(grads_kernel, out_shape=[jax.ShapeDtypeStruct((rows, colum...  283 us
    reduce_scatter x4, waiting for transfers between devices, low_scatter(): lax.psum_scatter(partial.astype(jnp.bfloat16), 'tensor', scatter_dimensio...  93.1 us
    dot_general x7, matrix products, times_cols(): lax.dot_general(left_side, right_side, (((1,), (1,)), ((), ())), preferre...  34.9 us
    dot_general x7, matrix products, product(): return jnp.dot(left_side, right_side, preferred_element_type=jnp.float32)  32.8 us
    all_gather x1, waiting for transfers between devices, body(): full_first = lax.all_gather(normed1, 'tensor', axis=0, tiled=True)  28.4 us
    all_gather x1, waiting for transfers between devices, body(): full_second = lax.all_gather(normed2, 'tensor', axis=0, tiled=True)  26.5 us
    convert_element_type x4, other arithmetic, body(): part.astype(jnp.float32)  24.9 us
    all_gather x1, waiting for transfers between devices, body(): lax.all_gather(grad_middle.astype(jnp.bfloat16), 'tensor', axis=0, tiled=...  18.1 us
  transfers between devices with their start and end apart: 8, of which 8 were waited for; matrix products, arithmetic and copies ran while one was open for 5% of the time, Pallas kernels for 0%

profile of v2, /device:TPU:0, one launch (start us, length us, event | category | flops | bytes accessed | tf_op | source)
XLA Modules:
  0.0 641.1 jit_solution(5670342285307222403)
XLA Ops:
  7.3 1.5 fusion.29
  9.3 2.3 fusion.18
  13.3 28.4 %all-gather.5.cloned.1.call-done.h1 = bf16[512,1536]{1,0:T(8,128)(2,1)} async-done(((bf16[256,1536]{1,0:T(8,128)(2,1)}), bf16[512,1536]{1,0:T(8,128)(2,1)}) %all-gather.5.cloned.1.call-update) | async-done | bytes 1572880 | tf_op jit(solution)/shard_map/all_gather | solution.py:537
  41.7 3.7 fusion.52
  47.7 1.7 fusion.50
  49.5 1.2 fusion.3
  52.8 1.6 fusion.33
  55.4 2.6 convolution_convert_fusion.1
  58.0 26.2 %reduce-scatter.5.cloned.1.call-done = bf16[256,1536]{1,0:T(8,128)(2,1)} async-done(((bf16[512,1536]{1,0:T(8,128)(2,1)}), bf16[256,1536]{1,0:T(8,128)(2,1)}) %reduce-scatter.5.cloned.1.call-update) | async-done | bytes 786448 | tf_op jit(solution)/shard_map/reduce_scatter | solution.py:514
  84.2 1.5 multiply_reduce_fusion.1
  85.8 1.2 multiply_convert_fusion.3
  87.9 26.5 %all-gather.7.cloned.1.call-done.h2 = bf16[512,1536]{1,0:T(8,128)(2,1)} async-done(((bf16[256,1536]{1,0:T(8,128)(2,1)}), bf16[512,1536]{1,0:T(8,128)(2,1)}) %all-gather.7.cloned.1.call-update) | async-done | bytes 1572880 | tf_op jit(solution)/shard_map/all_gather | solution.py:590
  114.4 8.8 %fusion.53 = f32[512,2048]{1,0:T(8,128)} fusion(bf16[512,1536]{1,0:T(8,128)(2,1)} %all-gather.7.cloned.1.call-done.h2, bf16[1536,2048]{1,0:T(8,128)(2,1)} %param.20), kind=kOutput, calls=%fused_computation.121 | convolution fusion | flops 3221225472 | bytes 12058624 | tf_op jit(solution)/shard_map/dot_general | solution.py:20
  123.2 8.2 %fusion.54 = f32[512,2048]{1,0:T(8,128)} fusion(bf16[512,1536]{1,0:T(8,128)(2,1)S(1)} %copy-done.42, bf16[1536,2048]{1,0:T(8,128)(2,1)} %param.21), kind=kOutput, calls=%fused_computation.122 | convolution fusion | flops 3221225472 | bytes 12058624 | tf_op jit(solution)/shard_map/dot_general | solution.py:20
  131.4 11.7 %all-gather.9.cloned.1.call-done.g = bf16[512,1536]{1,0:T(8,128)(2,1)} async-done(((bf16[256,1536]{1,0:T(8,128)(2,1)}), bf16[512,1536]{1,0:T(8,128)(2,1)}) %all-gather.9.cloned.1.call-update) | async-done | bytes 1572880 | tf_op jit(solution)/shard_map/all_gather | solution.py:604
  143.1 11.7 %multiply_convert_fusion = (bf16[512,2048]{1,0:T(8,128)(2,1)S(1)}, bf16[512,2048]{1,0:T(8,128)(2,1)S(1)}, bf16[512,2048]{1,0:T(8,128)(2,1)}) fusion(f32[512,2048]{1,0:T(8,128)} %fusion.53, f32[512,2048]{1,0:T(8,128)} %fusion.54, bf16[512,1536]{1,0:T(8,128)(2,1)} %all-gather.9.cloned.1.call-done.g, bf16[2048,1536]{1,0:T(8,128)(2,1)} %param.22), kind=kOutput, calls=%fused_computation.14 | convolution fusion | flops 3238002688 | bytes 22544384 | tf_op jit(solution)/shard_map/dot_general | solution.py:30
  154.8 7.3 %fusion.55 = f32[512,1536]{1,0:T(8,128)S(1)} fusion(bf16[512,2048]{1,0:T(8,128)(2,1)S(1)} %get-tuple-element.103.d_gate, bf16[1536,2048]{1,0:T(8,128)(2,1)} %param.20), kind=kOutput, calls=%fused_computation.123 | convolution fusion | flops 3221225472 | bytes 11534336 | tf_op jit(solution)/shard_map/dot_general | solution.py:30
  162.1 7.6 %fusion.12 = bf16[512,1536]{1,0:T(8,128)(2,1)} fusion(f32[512,1536]{1,0:T(8,128)S(1)} %fusion.55, bf16[512,2048]{1,0:T(8,128)(2,1)S(1)} %get-tuple-element.102.d_up, bf16[1536,2048]{1,0:T(8,128)(2,1)} %param.21), kind=kOutput, calls=%fused_computation.31 | convolution fusion | flops 3222798336 | bytes 13107200 | tf_op jit(solution)/shard_map/dot_general | solution.py:30
  169.7 8.0 %convolution_convert_fusion = bf16[512,1536]{1,0:T(8,128)(2,1)} fusion(bf16[512,2048]{1,0:T(8,128)(2,1)} %get-tuple-element.104.hid, bf16[2048,1536]{1,0:T(8,128)(2,1)} %param.22), kind=kOutput, calls=%fused_computation.29 | convolution fusion | flops 3222011904 | bytes 9961472 | tf_op jit(solution)/shard_map/dot_general | solution.py:20
  177.8 18.1 %reduce-scatter.9.cloned.1.call-done = bf16[256,1536]{1,0:T(8,128)(2,1)} async-done(((bf16[512,1536]{1,0:T(8,128)(2,1)}), bf16[256,1536]{1,0:T(8,128)(2,1)}) %reduce-scatter.9.cloned.1.call-update) | async-done | bytes 786448 | tf_op jit(solution)/shard_map/reduce_scatter | solution.py:514
  195.9 28.8 %reduce-scatter.7.cloned.1.call-done = bf16[256,1536]{1,0:T(8,128)(2,1)} async-done(((bf16[512,1536]{1,0:T(8,128)(2,1)}), bf16[256,1536]{1,0:T(8,128)(2,1)}) %reduce-scatter.7.cloned.1.call-update) | async-done | bytes 786448 | tf_op jit(solution)/shard_map/reduce_scatter | solution.py:514
  224.7 4.4 fusion.28
  229.2 1.6 fusion.48
  230.8 8.5 %reduce-scatter.11.cloned.1.call-start = ((), (), s32[]{:S(2)}) async-start(), calls=%async_computation.11 | async-start | bytes 2359296 | tf_op jit(solution)/shard_map/reduce_scatter | solution.py:514
  240.1 18.1 %all-gather.11.cloned.1.call-done.d_attn = bf16[512,1536]{1,0:T(8,128)(2,1)} async-done(((bf16[256,1536]{1,0:T(8,128)(2,1)}), bf16[512,1536]{1,0:T(8,128)(2,1)}) %all-gather.11.cloned.1.call-update) | async-done | bytes 1572880 | tf_op jit(solution)/shard_map/all_gather | solution.py:619
  258.2 3.7 convolution_convert_fusion.2
  261.9 1.4 copy.51
  263.3 5.1 fusion.39
  268.4 5.2 fusion
  273.6 2.6 fusion.2
  276.3 1.4 fusion.38
  279.1 1.3 copy-done.40
  280.4 1.4 fusion.56
  283.2 2.2 fusion.11
  287.7 2.0 select_maximum_fusion.2
  290.4 1.3 pad_maximum_fusion.d_qkv
  291.7 19.9 %reduce-scatter.11.cloned.1.call-done = bf16[256,1536]{1,0:T(8,128)(2,1)} async-done(((bf16[512,1536]{1,0:T(8,128)(2,1)}), bf16[256,1536]{1,0:T(8,128)(2,1)}) %reduce-scatter.11.cloned.1.call-update) | async-done | bytes 786448 | tf_op jit(solution)/shard_map/reduce_scatter | solution.py:514
  311.6 1.6 fusion.32
  313.9 282.6 %weight_grads.1 = (bf16[2048,1536]{1,0:T(8,128)(2,1)}, bf16[1536,2048]{1,0:T(8,128)(2,1)}, bf16[1536,2048]{1,0:T(8,128)(2,1)}, bf16[768,1536]{1,0:T(8,128)(2,1)}...) custom-call(bf16[512,2048]{1,0:T(8,128)(2,1)} %get-tuple-element.104.hid, ...), custom_call_target="tpu_custom_call" | custom-call | flops 13287555072 | bytes 83886080 | tf_op jit(solution)/shard_map/weight_grads/pallas_call | solution.py:482
  596.5 4.3 fusion.49
  600.8 2.7 slice.67
  603.5 1.7 slice_reduce_fusion
  605.2 1.2 sqrt_bitcast_fusion
  606.4 9.2 %convert_element_type.164 = f32[1536,2048]{1,0:T(8,128)} convert(bf16[1536,2048]{1,0:T(8,128)(2,1)} %get-tuple-element.77) | non-fusion elementwise | flops 3145728 | bytes 18874368 | tf_op jit(solution)/shard_map/convert_element_type | solution.py:686
  615.7 6.3 convert_element_type.165
  622.0 6.6 %convert_element_type.166 = f32[2048,1536]{1,0:T(8,128)} convert(bf16[2048,1536]{1,0:T(8,128)(2,1)S(1)} %bitcast.110) | non-fusion elementwise | flops 3145728 | bytes 18874368 | tf_op jit(solution)/shard_map/convert_element_type | solution.py:686
  628.6 2.8 convert_element_type.163
  631.5 2.3 fusion.21
  (153 shorter events, 15.7 us)
Async XLA Ops:
  7.2 48.2 %copy-start = (bf16[768,1536]{1,0:T(8,128)(2,1)S(1)}, bf16[768,1536]{1,0:T(8,128)(2,1)}, u32[]{:S(2)}) copy-start(bf16[768,1536]{1,0:T(8,128)(2,1)} %param.18) | copy-start | bytes 7077892
  7.2 4.5 copy-start.43
  7.2 34.5 %all-gather.5.cloned.1.call-start = ((), (), s32[]{:S(2)}) async-start(), calls=%async_computation.4 | async-start | bytes 2359296 | tf_op jit(solution)/shard_map/all_gather | solution.py:537
  11.6 72.6 %reduce-scatter.5.cloned.1.call-start = ((), (), s32[]{:S(2)}) async-start(), calls=%async_computation.5 | async-start | bytes 2359296 | tf_op jit(solution)/shard_map/reduce_scatter | solution.py:514
  41.7 4.0 copy-start.41
  47.6 1.8 copy-start.18
  47.6 1.8 copy-start.20
  47.7 1.7 copy-start.8
  49.4 3.4 copy-start.2
  49.4 2.1 copy-start.26
  51.6 2.9 copy-start.33
  52.4 2.1 copy-start.28
  55.4 28.8 %copy-start.3 = (bf16[256,1536]{1,0:T(8,128)(2,1)S(1)}, bf16[256,1536]{1,0:T(8,128)(2,1)}, u32[]{:S(2)}) copy-start(bf16[256,1536]{1,0:T(8,128)(2,1)} %param.12) | copy-start | bytes 2359300
  57.9 27.8 %copy-start.31 = (f32[1536]{0:T(1024)S(1)}, f32[1536]{0:T(1024)}, u32[]{:S(2)}) copy-start(f32[1536]{0:T(1024)} %param.19) | copy-start | bytes 18436
  58.0 56.4 %all-gather.7.cloned.1.call-start = ((), (), s32[]{:S(2)}) async-start(), calls=%async_computation.6 | async-start | bytes 2359296 | tf_op jit(solution)/shard_map/all_gather | solution.py:590
  85.8 143.4 %copy-start.34 = (f32[256]{0:T(256)}, f32[256]{0:T(256)S(1)}, u32[]{:S(2)}) copy-start(f32[256]{0:T(256)S(1)} %add_rsqrt_fusion) | copy-start | bytes 3076
  87.0 56.1 %all-gather.9.cloned.1.call-start = ((), (), s32[]{:S(2)}) async-start(), calls=%async_computation.8 | async-start | bytes 2359296 | tf_op jit(solution)/shard_map/all_gather | solution.py:604
  87.6 108.3 %reduce-scatter.9.cloned.1.call-start = ((), (), s32[]{:S(2)}) async-start(), calls=%async_computation.9 | async-start | bytes 2359296 | tf_op jit(solution)/shard_map/reduce_scatter | solution.py:514
  114.4 8.8 %copy-start.42 = (bf16[512,1536]{1,0:T(8,128)(2,1)S(1)}, bf16[512,1536]{1,0:T(8,128)(2,1)}, u32[]{:S(2)}) copy-start(bf16[512,1536]{1,0:T(8,128)(2,1)} %all-gather.7.cloned.1.call-done.h2) | copy-start | bytes 4718596
  154.8 7.3 %copy-start.45 = (bf16[512,2048]{1,0:T(8,128)(2,1)}, bf16[512,2048]{1,0:T(8,128)(2,1)S(1)}, u32[]{:S(2)}) copy-start(bf16[512,2048]{1,0:T(8,128)(2,1)S(1)} %get-tuple-element.103.d_gate) | copy-start | bytes 6291460
  154.8 7.3 %copy-start.44 = (bf16[512,2048]{1,0:T(8,128)(2,1)}, bf16[512,2048]{1,0:T(8,128)(2,1)S(1)}, u32[]{:S(2)}) copy-start(bf16[512,2048]{1,0:T(8,128)(2,1)S(1)} %get-tuple-element.102.d_up) | copy-start | bytes 6291460
  169.7 55.0 %reduce-scatter.7.cloned.1.call-start = ((), (), s32[]{:S(2)}) async-start(), calls=%async_computation.7 | async-start | bytes 2359296 | tf_op jit(solution)/shard_map/reduce_scatter | solution.py:514
  177.7 80.4 %all-gather.11.cloned.1.call-start = ((), (), s32[]{:S(2)}) async-start(), calls=%async_computation.10 | async-start | bytes 2359296 | tf_op jit(solution)/shard_map/all_gather | solution.py:619
  224.7 4.5 copy-start.5
  224.7 4.5 copy-start.10
  224.7 4.5 copy-start.12
  230.8 80.8 %reduce-scatter.11.cloned.1.call-start = ((), (), s32[]{:S(2)}) async-start(), calls=%async_computation.11 | async-start | bytes 2359296 | tf_op jit(solution)/shard_map/reduce_scatter | solution.py:514
  263.3 5.1 copy-start.29
  263.3 10.3 %slice-start = ((s8[8388608]{0:T(1024)(128)(4,1)}), s8[4194304]{0:T(1024)(128)(4,1)S(1)}, s32[]{:S(2)}) async-start(s8[8388608]{0:T(1024)(128)(4,1)} %bitcast.104), calls=%async_computation.12 | async-start | bytes 8388608
  268.4 14.6 %copy-start.22 = (bf16[4,96,512]{2,1,0:T(8,128)(2,1)}, bf16[4,96,512]{2,1,0:T(8,128)(2,1)S(1)}, u32[]{:S(2)}) copy-start(bf16[4,96,512]{2,1,0:T(8,128)(2,1)S(1)} %fusion.39) | copy-start | bytes 1179652
  268.4 5.2 slice-start.1
  273.6 2.6 copy-start.9
  285.4 4.3 copy-start.23
  290.1 21.5 %copy-start.32 = (f32[1536]{0:T(1024)S(1)}, f32[1536]{0:T(1024)}, u32[]{:S(2)}) copy-start(f32[1536]{0:T(1024)} %param.14) | copy-start | bytes 18436
  290.1 21.5 %copy-start.37 = (f32[256]{0:T(256)S(1)}, f32[256]{0:T(256)}, u32[]{:S(2)}) copy-start(f32[256]{0:T(256)} %copy-done.36) | copy-start | bytes 3076
  596.5 4.3 copy-start.7
  600.8 14.9 %slice-start.4 = ((s8[6291456]{0:T(1024)(128)(4,1)}), s8[4194304]{0:T(1024)(128)(4,1)S(1)}, s32[]{:S(2)}) async-start(s8[6291456]{0:T(1024)(128)(4,1)} %bitcast.111), calls=%async_computation.16 | async-start | bytes 8388608
  606.4 9.3 %slice-start.5 = ((s8[6291456]{0:T(1024)(128)(4,1)}), s8[2097152]{0:T(1024)(128)(4,1)S(1)}, s32[]{:S(2)}) async-start(s8[6291456]{0:T(1024)(128)(4,1)} %bitcast.111), calls=%async_computation.17 | async-start | bytes 4194304
  606.4 15.6 %slice-start.2 = ((s8[6291456]{0:T(1024)(128)(4,1)}), s8[4194304]{0:T(1024)(128)(4,1)S(1)}, s32[]{:S(2)}) async-start(s8[6291456]{0:T(1024)(128)(4,1)} %bitcast.109), calls=%async_computation.14 | async-start | bytes 8388608
  615.7 6.3 slice-start.3
  622.0 6.6 %copy-start.17 = (bf16[768,1536]{1,0:T(8,128)(2,1)S(1)}, bf16[768,1536]{1,0:T(8,128)(2,1)}, u32[]{:S(2)}) copy-start(bf16[768,1536]{1,0:T(8,128)(2,1)} %get-tuple-element.76) | copy-start | bytes 7077892
  628.6 2.9 copy-start.6
  628.6 2.9 copy-start.11
  628.6 2.9 copy-start.13
  628.6 2.9 copy-start.16
  628.6 2.9 copy-start.35
  628.6 2.9 copy-start.39
  631.4 2.4 copy-start.1
  (12 other events, 15.2 us)
Sparse Core Ops, SparseCore 0:
  11.8 29.8 all-gather.4
  58.1 26.0 reduce-scatter.4
  87.1 27.2 all-gather.6
  115.9 27.2 all-gather.8
  169.8 26.0 reduce-scatter.8
  198.6 26.0 reduce-scatter.6
  230.9 27.2 all-gather.10
  285.5 26.0 reduce-scatter.10

commit v3 on v2

--- a/solution.py
+++ b/solution.py
@@ -42,10 +42,11 @@
         (places[:, None] >= seq_ends[None, :]).astype(jnp.int32), axis=1, dtype=jnp.int32
     )
     member = segment[:, None] == jnp.arange(lens_row.shape[0], dtype=jnp.int32)[None, :]
-    position = places - jnp.sum(jnp.where(member, starts[None, :], 0), axis=1, dtype=jnp.int32)
+    firsts = jnp.sum(jnp.where(member, starts[None, :], 0), axis=1, dtype=jnp.int32)
+    position = places - firsts
     inverse = rope_base ** (-2.0 * jnp.arange(half_size, dtype=jnp.float32) / (2 * half_size))
     angles = position.astype(jnp.float32)[:, None] * inverse[None, :]
-    return (places, segment, jnp.cos(angles), jnp.sin(angles))
+    return (places, segment, jnp.cos(angles), jnp.sin(angles), firsts)
 
 
 def rotate(values, cosine_table, sine_table, direction):
@@ -75,11 +76,12 @@
 
 
 ORDER = (
-    0, 1, 5, 10, 11, 2, 6, 4, 11, 7, 3, 9, 14, 11, 8, 13, 10, 11, 11, 13, 13, 14, 11, 10, 13, 13,
-    11, 10, 13, 12, 13, 14, 18, 10, 14, 11, 13, 12, 14, 10, 11, 12, 13, 18, 19, 10, 14, 11, 11, 17,
-    12, 18, 16, 13, 13, 10, 10, 16, 19, 14, 18, 12, 19, 15, 14, 14, 17, 18, 16, 10, 17, 19, 19, 12,
-    16, 17, 17, 15, 12, 14, 16, 19, 17, 19, 12, 12, 17, 15, 18, 16, 19, 15, 15, 17, 18, 12, 16, 15,
-    19, 17, 18, 18, 15, 16, 16, 19, 19, 17, 17, 15, 18, 15, 16, 15, 15,
+    20, 0, 1, 5, 10, 11, 2, 6, 7, 11, 21, 11, 10, 13, 11, 11, 10, 12, 11, 22, 3, 10, 23, 8, 10, 13,
+    24, 25, 11, 13, 12, 10, 26, 27, 11, 28, 4, 13, 13, 12, 9, 10, 13, 15, 11, 13, 16, 10, 10, 12,
+    29, 11, 11, 15, 16, 14, 12, 30, 15, 31, 32, 10, 13, 16, 33, 34, 35, 15, 15, 12, 13, 16, 18, 14,
+    12, 15, 14, 13, 13, 16, 14, 12, 12, 16, 14, 18, 16, 15, 14, 19, 16, 16, 18, 14, 17, 18, 14, 14,
+    12, 15, 18, 19, 16, 15, 17, 19, 17, 18, 15, 15, 14, 19, 19, 17, 17, 19, 17, 18, 19, 17, 18, 18,
+    19, 17, 19, 17, 19, 19, 18, 17, 17,
 )
 
 
@@ -97,7 +99,8 @@
 TILES = tuple(rows // 2 // tile for rows, _, _, _, tile in UNITS)
 SMALL_BASE = TILE_BASE + sum(TILES)
 SMALL_STEPS = 5
-N_SEMS = SMALL_BASE + SMALL_STEPS
+Y_BASE = SMALL_BASE + SMALL_STEPS
+N_SEMS = Y_BASE + 4
 
 
 def rows_at(start, size):
@@ -181,6 +184,10 @@
         return 0
 
     lax.fori_loop(0, size // step, one, 0)
+
+
+def fall_slot(step):
+    return 0 if step == 0 else 2 + step
 
 
 class Block:
@@ -227,7 +234,7 @@
         p = self.p
         for step in range(3):
             self.m.start(self.part(3 - step), self.along.at[step], self.base + step, p.up(), p.z == 0)
-            self.m.start(self.part(step), self.along.at[3 + step], self.base + 3 + step, p.down(), p.z == LINE - 1)
+            self.m.start(self.part(step), self.along.at[fall_slot(step)], self.base + 3 + step, p.down(), p.z == LINE - 1)
 
     def line_add(self, step):
         p = self.p
@@ -241,15 +248,15 @@
             add_rows(self.held, self.origin + rising * self.chunk, self.along.at[step], 0, self.chunk)
 
         def take_falling():
-            self.m.arrived(self.along.at[3 + step], self.base + 3 + step, p.up())
-            add_rows(self.held, self.origin + falling * self.chunk, self.along.at[3 + step], 0, self.chunk)
+            self.m.arrived(self.along.at[fall_slot(step)], self.base + 3 + step, p.up())
+            add_rows(self.held, self.origin + falling * self.chunk, self.along.at[fall_slot(step)], 0, self.chunk)
 
         pl.when(goes_up)(take_rising)
         if step < 2:
             self.m.start(self.part(rising), self.along.at[step + 1], self.base + step + 1, p.up(), goes_up)
         pl.when(goes_down)(take_falling)
         if step < 2:
-            self.m.start(self.part(falling), self.along.at[4 + step], self.base + 4 + step, p.down(), goes_down)
+            self.m.start(self.part(falling), self.along.at[fall_slot(step + 1)], self.base + 4 + step, p.down(), goes_down)
         elif self.x_first:
             self.keep(self.origin + p.z * self.chunk, self.chunk)
             self.own_spread(self.part(p.z))
@@ -400,35 +407,228 @@
         lax.fori_loop(0, half // tile, one, 0)
 
 
+def row_scale(values):
+    return lax.rsqrt(jnp.mean(values * values, axis=-1, keepdims=True) + epsilon)
+
+
+def eight(values):
+    rows, columns = values.shape
+    return jnp.sum(values.reshape(rows // 8, 8, columns), axis=0)
+
+
+def turn_back(values, cosines, sines):
+    half = values.shape[1] // 2
+    swapped = jnp.concatenate([values[:, half:], values[:, :half]], axis=1)
+    return values * cosines + swapped * sines
+
+
+def nt(left_side, right_side):
+    return lax.dot_general(
+        left_side, right_side, (((1,), (1,)), ((), ())), preferred_element_type=jnp.float32
+    )
+
+
+def tn(left_side, right_side):
+    return lax.dot_general(
+        left_side, right_side, (((0,), (0,)), ((), ())), preferred_element_type=jnp.float32
+    )
+
+
+class Layer:
+    def __init__(self, place, mover, **refs):
+        self.p, self.m = place, mover
+        self.__dict__.update(refs)
+        self.rows = self.x1.shape[0]
+        self.mine = rows_at(place.y * self.rows, self.rows)
+        self.theirs = rows_at((1 - place.y) * self.rows, self.rows)
+
+    def load(self, source, target, index):
+        copy = pltpu.make_async_copy(source, target, self.local_sems.at[index])
+        copy.start()
+        return copy
+
+    def begin(self):
+        self.m.start(self.h2_parts.at[self.theirs], self.h2_in, Y_BASE, self.p.other_y())
+        self.hid_load = self.load(self.hid_hbm, self.hid, 0)
+        self.h_load = self.load(self.h2_hbm, self.hbuf, 1)
+        self.own_load = self.load(self.h2_parts.at[self.mine], self.own, 2)
+        self.out_load = self.load(self.out_w, self.wbuf.at[pl.ds(0, 768)], 3)
+
+    def tiles(self, step, body):
+        lax.fori_loop(0, self.rows // step, lambda i, _: (body(i * step, step), 0)[1], 0)
+
+    def middle(self):
+        self.own_load.wait()
+        self.m.arrived(self.h2_in, Y_BASE, self.p.other_y())
+        self.gains[...] = jnp.zeros_like(self.gains)
+
+        def body(start, step):
+            here = rows_at(start, step)
+            there = rows_at(self.p.y * self.rows + start, step)
+            d = self.own[here, :].astype(jnp.float32) + self.h2_in[here, :].astype(jnp.float32)
+            x1 = self.x1[here, :]
+            inv = row_scale(x1)
+            scaled = d * self.gain2[...]
+            inner = jnp.mean(scaled * x1, axis=-1, keepdims=True)
+            self.gains[1] += eight(d * x1 * inv)
+            d_x1 = self.g[there, :].astype(jnp.float32) + inv * (scaled - x1 * inv * inv * inner)
+            self.d_x1[here, :] = d_x1
+            self.d_attn[there, :] = d_x1.astype(jnp.bfloat16)
+
+        self.tiles(16, body)
+        own = self.d_attn.at[self.mine]
+        self.m.start(own, own, Y_BASE + 1, self.p.other_y())
+
+    def outward(self):
+        self.m.arrived(self.d_attn.at[self.theirs], Y_BASE + 1, self.p.other_y())
+        self.out_load.wait()
+        for part in range(3):
+            cut = slice(part * 256, (part + 1) * 256)
+            self.d_o[:, cut] = nt(self.d_attn[...], self.wbuf[cut, :]).astype(jnp.bfloat16)
+        self.w_loads = [
+            self.load(self.q_w, self.wbuf.at[:, pl.ds(0, 768)], 3),
+            self.load(self.k_w, self.wbuf.at[:, pl.ds(768, 384)], 4),
+            self.load(self.v_w, self.wbuf.at[:, pl.ds(1152, 384)], 5),
+        ]
+
+    def attention(self, key_head):
+        factor = HD ** (-0.5)
+        c = key_head * HD
+        keys, values = self.k[:, c : c + HD], self.v[:, c : c + HD]
+        block = 256
+        d_k = [jnp.zeros((block, HD), jnp.float32)] * 2
+        d_v = [jnp.zeros((block, HD), jnp.float32)] * 2
+        for head in (2 * key_head, 2 * key_head + 1):
+            h = head * HD
+            for i in range(2):
+                here = slice(i * block, (i + 1) * block)
+                n = block * (i + 1)
+                query, d_out = self.q[here, h : h + HD], self.d_o[here, h : h + HD]
+                column = lax.broadcasted_iota(jnp.int32, (block, n), 1)
+                row = lax.broadcasted_iota(jnp.int32, (block, n), 0) + i * block
+                allowed = (column <= row) & (column >= self.starts[here, :])
+                masked = jnp.where(allowed, nt(query, keys[:n]) * factor, masked_score)
+                exponent = jnp.exp(masked - jnp.max(masked, axis=1, keepdims=True))
+                weights = exponent / jnp.sum(exponent, axis=1, keepdims=True)
+                d_weights = nt(d_out, values[:n])
+                inner = jnp.sum(weights * d_weights, axis=1, keepdims=True)
+                d_scores = (weights * (d_weights - inner)).astype(jnp.bfloat16)
+                low = weights.astype(jnp.bfloat16)
+                d_query = jnp.dot(d_scores, keys[:n], preferred_element_type=jnp.float32) * factor
+                turned = turn_back(d_query, self.cosines[here, :], self.sines[here, :])
+                self.d_qkv[here, h : h + HD] = turned.astype(jnp.bfloat16)
+                for j in range(i + 1):
+                    cut = slice(j * block, (j + 1) * block)
+                    d_k[j] = d_k[j] + tn(d_scores[:, cut], query) * factor
+                    d_v[j] = d_v[j] + tn(low[:, cut], d_out)
+        for j in range(2):
+            cut = slice(j * block, (j + 1) * block)
+            turned = turn_back(d_k[j], self.cosines[cut, :], self.sines[cut, :])
+            self.d_qkv[cut, 768 + c : 768 + c + HD] = turned.astype(jnp.bfloat16)
+            self.d_qkv[cut, 1152 + c : 1152 + c + HD] = d_v[j].astype(jnp.bfloat16)
+
+    def h1_part(self, rows, put):
+        def body(i, _):
+            cut = pl.ds(pl.multiple_of(i * 256, 256), 256)
+            put(cut, nt(self.d_qkv[rows, 0:1536], self.wbuf[cut, :]))
+            return 0
+
+        lax.fori_loop(0, 6, body, 0)
+
+    def inward(self):
+        for copy in self.w_loads:
+            copy.wait()
+
+        def put(cut, got):
+            self.h1_out[:, cut] = got.astype(jnp.bfloat16)
+
+        self.h1_part(self.theirs, put)
+        self.m.start(self.h1_out, self.h1_in, Y_BASE + 2, self.p.other_y())
+
+    def mlp_send(self):
+        self.m.start(self.mlp_parts.at[self.theirs], self.mlp_in, Y_BASE + 3, self.p.other_y())
+        self.own_load = self.load(self.mlp_parts.at[self.mine], self.own, 2)
+
+    def finish(self):
+        def put(cut, got):
+            self.fbuf[:, cut] = got
+
+        self.h1_part(self.mine, put)
+        self.m.arrived(self.h1_in, Y_BASE + 2, self.p.other_y())
+
+        def body(start, step):
+            here = rows_at(start, step)
+            d = self.fbuf[here, :] + self.h1_in[here, :].astype(jnp.float32)
+            x = self.x[here, :].astype(jnp.float32)
+            inv = row_scale(x)
+            scaled = d * self.gain1[...]
+            inner = jnp.mean(scaled * x, axis=-1, keepdims=True)
+            self.gains[0] += eight(d * x * inv)
+            self.d_x1[here, :] = self.d_x1[here, :] + inv * (scaled - x * inv * inv * inner)
+
+        self.tiles(16, body)
+        copy = self.load(self.d_x1, self.tokens_out, 6)
+        self.m.left.append((None, copy.wait))
+
+    def layer_end(self):
+        self.own_load.wait()
+        self.m.arrived(self.mlp_in, Y_BASE + 3, self.p.other_y())
+
+        def body(start, step):
+            here = rows_at(start, step)
+            mlp = self.own[here, :].astype(jnp.float32) + self.mlp_in[here, :].astype(jnp.float32)
+            out = self.x1[here, :] + mlp
+            self.gains[2] += eight(out * out)
+            self.gains[3] += eight(mlp * mlp)
+            self.y_low[here, :] = out.astype(jnp.bfloat16)
+
+        self.tiles(16, body)
+        copy = self.load(self.y_low, self.layer_out, 7)
+        self.m.left.append((None, copy.wait))
+        self.totals[0] = jnp.zeros(self.totals.shape[1:], jnp.float32)
+        for row in range(4):
+            self.totals[0, row : row + 1, :] = jnp.sum(self.gains[row], axis=0, keepdims=True)
+        self.totals[0, 4:5, :] = self.attn_squares[...]
+
+
 def sum_small(place, mover, total, slots, step):
     device = (place.other_core, place.other_x, place.other_y, place.pair_z, place.far_z)[step]()
-    index = SMALL_BASE + step
-    copy = mover.copy(total.at[step], slots.at[step], index, device)
+    copy = mover.copy(total.at[step], slots.at[step], SMALL_BASE + step, device)
     copy.start()
     copy.wait()
     total[step + 1] = total[step] + slots[step]
 
 
-def grads_kernel(
-    hid, g, h2, d_gate, d_up, o, d_attn, h1, d_qkv, small,
-    down_out, gate_out, up_out, o_out, qkv_out, small_out,
-    held0, held1, held2, held3, held4, staged,
-    ax0, az0, ax1, az1, ax2, az2, ax3, az3, ax4, az4,
-    lx0, lz0, lx1, lz1, lx2, lz2, lx3, lz3, lx4, lz4,
-    totals, slots, stage_sems, send_sems, recv_sems, keep_sems,
-):
+INPUTS = (
+    "hid_hbm", "g", "h2_hbm", "d_gate", "d_up", "o", "h1_hbm", "q", "k", "v", "out_w", "q_w", "k_w", "v_w",
+    "x1", "x", "h2_parts", "mlp_parts", "cosines", "sines", "starts", "gain1", "gain2", "attn_squares",
+)
+IN_HBM = ("hid_hbm", "h2_hbm", "h1_hbm", "out_w", "q_w", "k_w", "v_w", "h2_parts", "mlp_parts")
+RESULTS = ("down_out", "gate_out", "up_out", "o_out", "qkv_out", "tokens_out", "layer_out", "small_out")
+PLAIN = (
+    "staged", "hid", "hbuf", "own", "h2_in", "d_attn", "d_x1", "wbuf", "d_o", "h1_out", "h1_in", "mlp_in",
+    "y_low", "fbuf", "gains", "totals", "slots", "stage_sems", "send_sems", "recv_sems", "keep_sems", "local_sems",
+)
+
+
+def backward_kernel(*refs):
+    n = len(UNITS)
+    names = INPUTS + RESULTS
+    r = dict(zip(names, refs[: len(names)]))
+    rest = refs[len(names) :]
+    held, across, along = rest[:n], rest[n : 3 * n], rest[3 * n : 5 * n]
+    r.update(zip(PLAIN, rest[5 * n :]))
+    r["d_qkv"] = r["hid"]
     place = Place()
-    mover = Mover(send_sems, recv_sems)
-    mover.keep_sems = keep_sems
+    mover = Mover(r["send_sems"], r["recv_sems"])
+    mover.keep_sems = r["keep_sems"]
     enter(place)
-    held = (held0, held1, held2, held3, held4)
-    across = (ax0, az0, ax1, az1, ax2, az2, ax3, az3, ax4, az4)
-    along = (lx0, lz0, lx1, lz1, lx2, lz2, lx3, lz3, lx4, lz4)
-    lefts = (hid, h2, h2, o, h1)
-    rights = (g, d_gate, d_up, d_attn, d_qkv)
-    results = (down_out, gate_out, up_out, o_out, qkv_out)
+    layer = Layer(place, mover, **r)
+    lefts = (r["hid"], r["hbuf"], r["hbuf"], r["o"], r["hbuf"])
+    rights = (r["g"], r["d_gate"], r["d_up"], r["d_attn"], r["d_qkv"])
+    results = tuple(r[name] for name in RESULTS[:n])
     units = [
-        Unit(i, place, mover, lefts[i], rights[i], held[i], staged, stage_sems) for i in range(len(UNITS))
+        Unit(i, place, mover, lefts[i], rights[i], held[i], r["staged"], r["stage_sems"]) for i in range(n)
     ]
     steps = []
     for i, (rows, columns, x_rows, z_rows, _) in enumerate(UNITS):
@@ -439,19 +639,31 @@
                 0 if j == 0 else x_rows, x_rows if j == 0 else z_rows, rows // 2, j == 0,
             )
             steps.append(block.events())
-    totals[0] = small[...]
-    small_at = 0
-    for count, item in enumerate(ORDER):
+
+    def send(i):
+        if i == 0:
+            layer.hid_load.wait()
+        if i == 1:
+            layer.h_load.wait()
+        if i == 4:
+            layer.h_load = layer.load(layer.h1_hbm, layer.hbuf, 1)
+            layer.h_load.wait()
+        units[i].send()
+
+    tasks = [layer.begin, layer.middle, layer.outward]
+    tasks += [partial(layer.attention, i) for i in range(4)]
+    tasks += [layer.inward, layer.mlp_send, layer.finish, layer.layer_end]
+    tasks += [partial(sum_small, place, mover, r["totals"], r["slots"], i) for i in range(SMALL_STEPS)]
+    for item in ORDER:
         if item < 5:
-            units[item].send()
+            send(item)
         elif item < 10:
             units[item - 5].own()
+        elif item < 20:
+            steps[item - 10].pop(0)()
         else:
-            steps[item - 10].pop(0)()
-        if count % 8 == 7 and small_at < SMALL_STEPS:
-            sum_small(place, mover, totals, slots, small_at)
-            small_at += 1
-    small_out[...] = totals[SMALL_STEPS]
+            tasks[item - 20]()
+    r["small_out"][...] = r["totals"][SMALL_STEPS]
     for when, wait in mover.left:
         guarded(when, wait)
 
@@ -469,40 +681,59 @@
     pl.semaphore_wait(barrier, 5 + jnp.where(middle, 1, 0))
 
 
-def weight_grads(hid, g, h2, d_gate, d_up, o, d_attn, h1, d_qkv, small):
+def backward(**given):
     vmem = pl.BlockSpec(memory_space=pltpu.VMEM)
     hbm = pl.BlockSpec(memory_space=pl.ANY)
-    low = jnp.bfloat16
+    low, full = jnp.bfloat16, jnp.float32
+    own_rows, width = given["x1"].shape
     held = [pltpu.VMEM((rows // 2, columns), low) for rows, columns, *_ in UNITS]
     across, along = [], []
     for _, columns, x_rows, z_rows, _ in UNITS:
         across += [pltpu.VMEM((x_rows // 2, columns), low), pltpu.VMEM((z_rows // 8, columns), low)]
-        along += [pltpu.VMEM((6, x_rows // 8, columns), low), pltpu.VMEM((6, z_rows // 4, columns), low)]
+        along += [pltpu.VMEM((5, x_rows // 8, columns), low), pltpu.VMEM((5, z_rows // 4, columns), low)]
+    part = pltpu.VMEM((own_rows, width), low)
+    plain = dict(
+        staged=pltpu.VMEM((2, 256, 2048), low),
+        hid=pltpu.VMEM((512, 2048), low),
+        hbuf=pltpu.VMEM((512, width), low),
+        own=part,
+        h2_in=part,
+        d_attn=pltpu.VMEM((512, width), low),
+        d_x1=pltpu.VMEM((own_rows, width), full),
+        wbuf=pltpu.VMEM((1536, 1536), low),
+        d_o=pltpu.VMEM((512, 768), low),
+        h1_out=part,
+        h1_in=part,
+        mlp_in=part,
+        y_low=part,
+        fbuf=pltpu.VMEM((own_rows, width), full),
+        gains=pltpu.VMEM((4, 8, width), full),
+        totals=pltpu.VMEM((SMALL_STEPS + 1, 8, width), full),
+        slots=pltpu.VMEM((SMALL_STEPS, 8, width), full),
+        stage_sems=pltpu.SemaphoreType.DMA((2,)),
+        send_sems=pltpu.SemaphoreType.DMA((N_SEMS,)),
+        recv_sems=pltpu.SemaphoreType.DMA((N_SEMS,)),
+        keep_sems=pltpu.SemaphoreType.DMA((2 * len(UNITS),)),
+        local_sems=pltpu.SemaphoreType.DMA((8,)),
+    )
     flops = sum(2 * 512 * rows * columns for rows, columns, *_ in UNITS)
     return pl.pallas_call(
-        grads_kernel,
+        backward_kernel,
         out_shape=[jax.ShapeDtypeStruct((rows, columns), low) for rows, columns, *_ in UNITS]
-        + [jax.ShapeDtypeStruct(small.shape, jnp.float32)],
-        in_specs=[vmem] * 10,
-        out_specs=[hbm] * 5 + [vmem],
-        scratch_shapes=held
-        + [pltpu.VMEM((2, 256, 2048), low)]
-        + across
-        + along
         + [
-            pltpu.VMEM((SMALL_STEPS + 1,) + small.shape, jnp.float32),
-            pltpu.VMEM((SMALL_STEPS,) + small.shape, jnp.float32),
-            pltpu.SemaphoreType.DMA((2,)),
-            pltpu.SemaphoreType.DMA((N_SEMS,)),
-            pltpu.SemaphoreType.DMA((N_SEMS,)),
-            pltpu.SemaphoreType.DMA((2 * len(UNITS),)),
+            jax.ShapeDtypeStruct((own_rows, width), full),
+            jax.ShapeDtypeStruct((own_rows, width), low),
+            jax.ShapeDtypeStruct((8, width), full),
         ],
+        in_specs=[hbm if name in IN_HBM else vmem for name in INPUTS],
+        out_specs=[hbm] * 7 + [vmem],
+        scratch_shapes=held + across + along + [plain[name] for name in PLAIN],
         compiler_params=pltpu.CompilerParams(
-            collective_id=0, has_side_effects=True, vmem_limit_bytes=60 << 20
+            collective_id=0, has_side_effects=True, vmem_limit_bytes=62 << 20
         ),
         cost_estimate=pl.CostEstimate(flops=flops, bytes_accessed=80 << 20, transcendentals=0),
-        name="weight_grads",
-    )(hid, g, h2, d_gate, d_up, o, d_attn, h1, d_qkv, small)
+        name="backward",
+    )(*(given[name] for name in INPUTS))
 
 
 def dp_sum(terms):
@@ -517,7 +748,6 @@
 
 
 def body(
-    fused,
     tokens,
     lengths,
     first_gain,
@@ -536,7 +766,7 @@
     normed1 = normed1.astype(jnp.bfloat16)
     full_first = lax.all_gather(normed1, "tensor", axis=0, tiled=True)
     total_rows = full_first.shape[0]
-    places, segment, cosine_table, sine_table = tables(lengths[0], total_rows, HD // 2)
+    places, segment, cosine_table, sine_table, _ = tables(lengths[0], total_rows, HD // 2)
     kv_heads = key_weight.shape[1] // HD
     groups = query_weight.shape[1] // key_weight.shape[1]
     query = rotate(product(full_first, query_weight), cosine_table, sine_table, 1.0).astype(
@@ -609,8 +839,7 @@
     grad_up = (grad_hidden * gate_value * gate_sig).astype(jnp.bfloat16)
     gate_g = times_rows(full_second, grad_gate)
     up_g = times_rows(full_second, grad_up)
-    if not fused:
-        gate_g, up_g, down_g = dp_sum((gate_g, up_g, down_g))
+    gate_g, up_g, down_g = dp_sum((gate_g, up_g, down_g))
     grad_normed2 = low_scatter(
         times_cols(grad_gate, gate_weight) + times_cols(grad_up, up_weight)
     )
@@ -674,24 +903,8 @@
     first_rows, grad_in_norm = norm_back(inputs, inv_first, first_gain, grad_normed1)
     tokens_grad = grad_middle + grad_in_norm
     gain_rows = jnp.stack([first_rows, second_rows])
-    if fused:
-        small = jnp.concatenate(
-            [gain_rows, jnp.pad(squares, (0, gain_rows.shape[1] - 3))[None]], axis=0
-        )
-        small = jnp.pad(small, ((0, 5), (0, 0)))
-        *sums, small = weight_grads(
-            hidden, grad_full, full_second, grad_gate, grad_up, attended, grad_attn_full, full_first,
-            jnp.concatenate([query_lin, key_lin, value_lin], axis=1), small,
-        )
-        down_g, gate_g, up_g, output_g, qkv_g = (part.astype(jnp.float32) for part in sums)
-        q_cols, k_cols = query_lin.shape[1], key_lin.shape[1]
-        query_g = qkv_g[:, :q_cols]
-        key_g = qkv_g[:, q_cols : q_cols + k_cols]
-        value_g = qkv_g[:, q_cols + k_cols :]
-        gain_rows, squares = small[:2], small[2, :3]
-    else:
-        query_g, key_g, value_g, output_g = dp_sum((query_g, key_g, value_g, output_g))
-        gain_rows, squares = lax.psum((gain_rows, squares), ("dp", "tensor"))
+    query_g, key_g, value_g, output_g = dp_sum((query_g, key_g, value_g, output_g))
+    gain_rows, squares = lax.psum((gain_rows, squares), ("dp", "tensor"))
     rms_values = jnp.sqrt(squares / (total_rows * lax.axis_size("dp")))
     return (
         layer_out.astype(jnp.bfloat16),
@@ -709,6 +922,117 @@
     )
 
 
+def fused_body(
+    tokens,
+    lengths,
+    first_gain,
+    query_weight,
+    key_weight,
+    value_weight,
+    output_weight,
+    second_gain,
+    gate_weight,
+    up_weight,
+    down_weight,
+    out_cotangent,
+):
+    inputs = tokens.astype(jnp.float32)
+    normed1, _ = norm_rows(inputs, first_gain)
+    full_first = lax.all_gather(normed1.astype(jnp.bfloat16), "tensor", axis=0, tiled=True)
+    total_rows = full_first.shape[0]
+    places, segment, cosine_table, sine_table, firsts = tables(lengths[0], total_rows, HD // 2)
+    kv_heads = key_weight.shape[1] // HD
+    groups = query_weight.shape[1] // key_weight.shape[1]
+    query = rotate(product(full_first, query_weight), cosine_table, sine_table, 1.0).astype(
+        jnp.bfloat16
+    )
+    keys = rotate(product(full_first, key_weight), cosine_table, sine_table, 1.0).astype(
+        jnp.bfloat16
+    )
+    values = product(full_first, value_weight).astype(jnp.bfloat16)
+    raw = jnp.einsum(
+        "qcgd,kcd->cgqk",
+        query.reshape(total_rows, kv_heads, groups, HD),
+        keys.reshape(total_rows, kv_heads, HD),
+        preferred_element_type=jnp.float32,
+    ) * HD ** (-0.5)
+    allowed = (segment[:, None] == segment[None, :]) & (places[:, None] >= places[None, :])
+    masked = jnp.where(allowed[None, None], raw, masked_score)
+    exponent = jnp.exp(masked - jnp.max(masked, axis=-1, keepdims=True))
+    weights = exponent / jnp.sum(exponent, axis=-1, keepdims=True)
+    attended = (
+        jnp.einsum(
+            "cgqk,kcd->qcgd",
+            weights.astype(jnp.bfloat16),
+            values.reshape(total_rows, kv_heads, HD),
+            preferred_element_type=jnp.float32,
+        )
+        .reshape(total_rows, -1)
+        .astype(jnp.bfloat16)
+    )
+    attn_rows = low_scatter(product(attended, output_weight))
+    middle = inputs + attn_rows
+    normed2, _ = norm_rows(middle, second_gain)
+    full_second = lax.all_gather(normed2.astype(jnp.bfloat16), "tensor", axis=0, tiled=True)
+    gate_value = product(full_second, gate_weight)
+    upward = product(full_second, up_weight)
+    gate_sig = jax.nn.sigmoid(gate_value)
+    hidden = (gate_value * gate_sig * upward).astype(jnp.bfloat16)
+    mlp_parts = product(hidden, down_weight).astype(jnp.bfloat16)
+    grad_full = lax.all_gather(out_cotangent, "tensor", axis=0, tiled=True)
+    grad_hidden = times_cols(grad_full, down_weight)
+    gate_slope = gate_sig * (1.0 + gate_value * (1.0 - gate_sig))
+    grad_gate = (grad_hidden * upward * gate_slope).astype(jnp.bfloat16)
+    grad_up = (grad_hidden * gate_value * gate_sig).astype(jnp.bfloat16)
+    h2_parts = (times_cols(grad_gate, gate_weight) + times_cols(grad_up, up_weight)).astype(
+        jnp.bfloat16
+    )
+    *sums, tokens_grad, layer_out, small = backward(
+        hid_hbm=hidden,
+        g=grad_full,
+        h2_hbm=full_second,
+        d_gate=grad_gate,
+        d_up=grad_up,
+        o=attended,
+        h1_hbm=full_first,
+        q=query,
+        k=keys,
+        v=values,
+        out_w=output_weight,
+        q_w=query_weight,
+        k_w=key_weight,
+        v_w=value_weight,
+        x1=middle,
+        x=tokens,
+        h2_parts=h2_parts,
+        mlp_parts=mlp_parts,
+        cosines=jnp.concatenate([cosine_table, cosine_table], axis=1),
+        sines=jnp.concatenate([sine_table, -sine_table], axis=1),
+        starts=firsts[:, None],
+        gain1=first_gain[None],
+        gain2=second_gain[None],
+        attn_squares=jnp.sum(attn_rows * attn_rows, axis=0)[None],
+    )
+    down_g, gate_g, up_g, output_g, qkv_g = (part.astype(jnp.float32) for part in sums)
+    q_cols, k_cols = query.shape[1], keys.shape[1]
+    squares = jnp.stack([jnp.sum(small[2]), jnp.sum(small[4]), jnp.sum(small[3])])
+    rms_values = jnp.sqrt(squares / (total_rows * lax.axis_size("dp")))
+    return (
+        layer_out,
+        tokens_grad,
+        small[0],
+        qkv_g[:, :q_cols],
+        qkv_g[:, q_cols : q_cols + k_cols],
+        qkv_g[:, q_cols + k_cols :],
+        output_g,
+        small[1],
+        gate_g,
+        up_g,
+        down_g,
+        rms_values,
+    )
+
+
 def solution(mesh):
     in_specs = (
         P(("dp", "tensor"), None),
@@ -739,4 +1063,5 @@
         P(),
     )
     fused = dict(mesh.shape) == {"dp": 16, "tensor": 2}
-    return jax.shard_map(partial(body, fused), mesh=mesh, in_specs=in_specs, out_specs=out_specs, check_vma=False)
+    chosen = fused_body if fused else body
+    return jax.shard_map(chosen, mesh=mesh, in_specs=in_specs, out_specs=out_specs, check_vma=False)

time: 649 us -> 511 us (0.79)
  waiting for transfers between devices: 178 us -> 85.6 us
  matrix products: 83.5 us -> 65.1 us
  other arithmetic: 53.6 us -> 37.2 us
  starting transfers between devices: 9.06 us -> 0.63 us
    reduce_scatter x4 -> x1, waiting for transfers between devices: 93.1 us -> 26.2 us  [low_scatter(): lax.psum_scatter(partial.astype(jnp.bfloat16), 'tensor', scatter_dimensio...]
    all_gather x4 -> x3, waiting for transfers between devices: 84.7 us -> 59.4 us  [the longest x1 27.6 us: fused_body(): lax.all_gather(normed1.astype(jnp.bfloat16), 'tensor', axis=0, tiled=True)]
    dot_general x7 -> x3, matrix products: 34.9 us -> 23.1 us  [times_cols(): lax.dot_general(left_side, right_side, (((1,), (1,)), ((), ())), preferre...]
    dot_general x6 -> x1, matrix products: 15.8 us -> 4.34 us  [fused_body(): jnp.einsum('cgqk,kcd->qcgd', weights.astype(jnp.bfloat16), values.reshape...]
    reduce_scatter x4 -> x1, starting transfers between devices: 8.9 us -> 0.04 us  [low_scatter(): lax.psum_scatter(partial.astype(jnp.bfloat16), 'tensor', scatter_dimensio...]
    convert_element_type x8, other arithmetic: 32.6 us -> 25.5 us  [the longest x4 22 us: fused_body(): part.astype(jnp.float32)]
  transfers between devices with their start and end apart: 8 -> 4, of which waited for: 8 -> 4; matrix products, arithmetic and copies ran while one was open for 5% -> 5% of each run, Pallas kernels for 0% -> 0%
where the time goes in v3:
time: 511 us; the launch traced here: 504 us
  Pallas kernels  283 us (55%)
  waiting for transfers between devices  85.6 us (17%)
  matrix products  65.1 us (13%)
  other arithmetic  37.2 us (7%)
  local copies, waits for them, and re-layouts  18.3 us (4%)
  between operations  14.5 us (3%)
    pallas_call x1, Pallas kernels, backward(): pl.pallas_call(backward_kernel, out_shape=[jax.ShapeDtypeStruct((rows, co...  283 us
    dot_general x7, matrix products, product(): return jnp.dot(left_side, right_side, preferred_element_type=jnp.float32)  32.2 us
    all_gather x1, waiting for transfers between devices, fused_body(): lax.all_gather(normed1.astype(jnp.bfloat16), 'tensor', axis=0, tiled=True)  27.6 us
    reduce_scatter x1, waiting for transfers between devices, low_scatter(): lax.psum_scatter(partial.astype(jnp.bfloat16), 'tensor', scatter_dimensio...  26.2 us
    dot_general x3, matrix products, times_cols(): lax.dot_general(left_side, right_side, (((1,), (1,)), ((), ())), preferre...  23.1 us
    convert_element_type x4, other arithmetic, fused_body(): part.astype(jnp.float32)  22 us
    all_gather x1, waiting for transfers between devices, fused_body(): lax.all_gather(normed2.astype(jnp.bfloat16), 'tensor', axis=0, tiled=True)  19.8 us
    all_gather x1, waiting for transfers between devices, fused_body(): grad_full = lax.all_gather(out_cotangent, 'tensor', axis=0, tiled=True)  11.9 us
  transfers between devices with their start and end apart: 4, of which 4 were waited for; matrix products, arithmetic and copies ran while one was open for 5% of the time, Pallas kernels for 0%

profile of v3, /device:TPU:0, one launch (start us, length us, event | category | flops | bytes accessed | tf_op | source)
XLA Modules:
  0.0 504.2 jit_solution(12083865507103622075)
XLA Ops:
  7.2 1.4 fusion.8
  8.6 2.3 fusion.10
  11.3 1.0 fusion.22
  12.5 0.9 fusion.12
  13.4 27.6 %all-gather.4.cloned.1.call-done.refs_6_ = bf16[512,1536]{1,0:T(8,128)(2,1)} async-done(((bf16[256,1536]{1,0:T(8,128)(2,1)}), bf16[512,1536]{1,0:T(8,128)(2,1)}) %all-gather.4.cloned.1.call-update) | async-done | bytes 1572880 | tf_op jit(solution)/shard_map/all_gather | solution.py:941
  41.0 3.7 fusion.34
  44.6 0.3 multiply_subtract_fusion
  44.9 1.1 copy-done.16
  46.0 0.8 fusion.33
  47.0 0.3 copy-done.18
  47.3 1.0 convolution_convert_fusion.2.refs_9_
  48.5 0.6 copy-done.8
  49.1 0.3 copy-done.9
  49.4 5.4 %fusion.28 = (f32[4,2,512]{2,1,0:T(2,128)S(1)}, f32[4,2,512,512]{2,3,1,0:T(8,128)}) fusion(pred[512,512]{0,1:T(8,128)(4,1)S(1)} %copy-done.9, bf16[512,4,2,96]{0,3,2,1:T(8,128)(2,1)S(1)} %bitcast.79, bf16[512,4,48]{0,2,1:T(8,128)(2,1)S(1)} %get-tuple-element.44, bf16[512,4,48]{0,2,1:T(8,128)(2,1)S(1)} %get-tuple-element.43), kind=kOutput, calls=%fused_computation.68 | convolution fusion | flops 411828736 | bytes 9846784 | tf_op jit(solution)/shard_map/sub | solution.py:961
  54.8 4.3 fusion.11
  59.2 2.6 convolution_convert_fusion.1
  61.8 26.2 %reduce-scatter.2.cloned.1.call-done = bf16[256,1536]{1,0:T(8,128)(2,1)} async-done(((bf16[512,1536]{1,0:T(8,128)(2,1)}), bf16[256,1536]{1,0:T(8,128)(2,1)}) %reduce-scatter.2.cloned.1.call-update) | async-done | bytes 786448 | tf_op jit(solution)/shard_map/reduce_scatter | solution.py:745
  88.0 3.3 fusion.7
  91.3 1.2 multiply_convert_fusion.3
  92.6 0.5 all-gather.8.cloned.1.call-start
  93.2 0.6 broadcast_in_dim.82.refs_21_
  93.8 0.6 broadcast_in_dim.83.refs_22_
  94.4 1.0 pad_maximum_fusion
  95.4 0.8 copy.68.refs_20_
  96.2 1.2 copy.65.refs_5_
  97.4 0.9 copy.67.refs_8_
  98.3 1.2 copy.66.refs_7_
  99.5 0.6 broadcast_in_dim.84.refs_23_
  100.1 19.8 %all-gather.6.cloned.1.call-done.refs_2_ = bf16[512,1536]{1,0:T(8,128)(2,1)} async-done(((bf16[256,1536]{1,0:T(8,128)(2,1)}), bf16[512,1536]{1,0:T(8,128)(2,1)}) %all-gather.6.cloned.1.call-update) | async-done | bytes 1572880 | tf_op jit(solution)/shard_map/all_gather | solution.py:976
  120.0 8.8 %fusion.35 = f32[512,2048]{1,0:T(8,128)} fusion(bf16[512,1536]{1,0:T(8,128)(2,1)} %all-gather.6.cloned.1.call-done.refs_2_, bf16[1536,2048]{1,0:T(8,128)(2,1)} %param.20), kind=kOutput, calls=%fused_computation.71 | convolution fusion | flops 3221225472 | bytes 12058624 | tf_op jit(solution)/shard_map/dot_general | solution.py:20
  128.8 8.0 %fusion.36 = f32[512,2048]{1,0:T(8,128)} fusion(bf16[512,1536]{1,0:T(8,128)(2,1)S(1)} %copy-done.17, bf16[1536,2048]{1,0:T(8,128)(2,1)} %param.21), kind=kOutput, calls=%fused_computation.72 | convolution fusion | flops 3221225472 | bytes 12058624 | tf_op jit(solution)/shard_map/dot_general | solution.py:20
  136.7 11.9 %all-gather.8.cloned.1.call-done.refs_1_ = bf16[512,1536]{1,0:T(8,128)(2,1)} async-done(((bf16[256,1536]{1,0:T(8,128)(2,1)}), bf16[512,1536]{1,0:T(8,128)(2,1)}) %all-gather.8.cloned.1.call-update) | async-done | bytes 1572880 | tf_op jit(solution)/shard_map/all_gather | solution.py:982
  148.7 10.3 %multiply_convert_fusion = (bf16[512,2048]{1,0:T(8,128)(2,1)S(1)}, bf16[512,2048]{1,0:T(8,128)(2,1)S(1)}, bf16[512,2048]{1,0:T(8,128)(2,1)S(1)}) fusion(f32[512,2048]{1,0:T(8,128)} %fusion.35, f32[512,2048]{1,0:T(8,128)} %fusion.36, bf16[512,1536]{1,0:T(8,128)(2,1)} %all-gather.8.cloned.1.call-done.refs_1_, bf16[2048,1536]{1,0:T(8,128)(2,1)} %param.22), kind=kOutput, calls=%fused_computation.5 | convolution fusion | flops 3238002688 | bytes 22544384 | tf_op jit(solution)/shard_map/dot_general | solution.py:30
  159.1 8.0 %fusion.37 = f32[512,1536]{1,0:T(8,128)S(1)} fusion(bf16[512,2048]{1,0:T(8,128)(2,1)S(1)} %get-tuple-element.36.refs_3_, bf16[1536,2048]{1,0:T(8,128)(2,1)} %param.20), kind=kOutput, calls=%fused_computation.73 | convolution fusion | flops 3221225472 | bytes 11534336 | tf_op jit(solution)/shard_map/dot_general | solution.py:30
  167.1 7.5 %convolution_convert_fusion.refs_17_ = bf16[512,1536]{1,0:T(8,128)(2,1)} fusion(bf16[512,2048]{1,0:T(8,128)(2,1)S(1)} %get-tuple-element.37.refs_0_, bf16[2048,1536]{1,0:T(8,128)(2,1)} %param.22), kind=kOutput, calls=%fused_computation.14 | convolution fusion | flops 3222011904 | bytes 9961472 | tf_op jit(solution)/shard_map/dot_general | solution.py:20
  174.6 4.8 fusion.6.refs_16_
  179.3 282.8 %backward.1 = (bf16[2048,1536]{1,0:T(8,128)(2,1)}, bf16[1536,2048]{1,0:T(8,128)(2,1)}, bf16[1536,2048]{1,0:T(8,128)(2,1)}, bf16[768,1536]{1,0:T(8,128)(2,1)}, bf...) custom-call(bf16[512,2048]{1,0:T(8,128)(2,1)} %copy-done.23, ...), custom_call_target="tpu_custom_call" | custom-call | flops 13287555072 | bytes 83886080 | tf_op jit(solution)/shard_map/backward/pallas_call | solution.py:720
  462.2 4.5 fusion.27
  466.7 2.7 slice.52
  469.4 0.7 slice_reduce_fusion.2
  470.1 0.4 copy-done.2
  470.6 6.3 %convert_element_type.104 = f32[1536,2048]{1,0:T(8,128)} convert(bf16[1536,2048]{1,0:T(8,128)(2,1)S(1)} %copy-done.2) | non-fusion elementwise | flops 3145728 | bytes 18874368 | tf_op jit(solution)/shard_map/convert_element_type | solution.py:1016
  476.9 6.3 %convert_element_type.105 = f32[1536,2048]{1,0:T(8,128)} convert(bf16[1536,2048]{1,0:T(8,128)(2,1)S(1)} %bitcast.76) | non-fusion elementwise | flops 3145728 | bytes 18874368 | tf_op jit(solution)/shard_map/convert_element_type | solution.py:1016
  483.2 6.6 %convert_element_type.106 = f32[2048,1536]{1,0:T(8,128)} convert(bf16[2048,1536]{1,0:T(8,128)(2,1)S(1)} %bitcast.74) | non-fusion elementwise | flops 3145728 | bytes 18874368 | tf_op jit(solution)/shard_map/convert_element_type | solution.py:1016
  489.8 2.8 convert_element_type.103
  492.6 2.6 fusion.23
  495.2 0.9 copy.76
  496.1 1.1 copy.77
  (79 shorter events, 1.3 us)
Async XLA Ops:
  7.2 3.8 copy-start.20
  7.2 33.8 %all-gather.4.cloned.1.call-start = ((), (), s32[]{:S(2)}) async-start(), calls=%async_computation.1 | async-start | bytes 2359296 | tf_op jit(solution)/shard_map/all_gather | solution.py:941
  10.9 77.1 %reduce-scatter.2.cloned.1.call-start = ((), (), s32[]{:S(2)}) async-start(), calls=%async_computation.2 | async-start | bytes 2359296 | tf_op jit(solution)/shard_map/reduce_scatter | solution.py:745
  11.2 1.0 copy-start.14
  41.0 3.9 copy-start.19
  44.6 1.4 copy-start.16
  46.0 1.3 copy-start.18
  48.3 0.8 copy-start.8
  48.3 1.1 copy-start.9
  54.8 4.3 copy-start.5
  59.2 28.8 %copy-start.1 = (bf16[256,1536]{1,0:T(8,128)(2,1)S(1)}, bf16[256,1536]{1,0:T(8,128)(2,1)}, u32[]{:S(2)}) copy-start(bf16[256,1536]{1,0:T(8,128)(2,1)} %refs_15_.1) | copy-start | bytes 2359300
  61.8 29.6 %copy-start.11 = (f32[1536]{0:T(1024)S(1)}, f32[1536]{0:T(1024)}, u32[]{:S(2)}) copy-start(f32[1536]{0:T(1024)} %param.19) | copy-start | bytes 18436
  61.8 58.2 %all-gather.6.cloned.1.call-start = ((), (), s32[]{:S(2)}) async-start(), calls=%async_computation.3 | async-start | bytes 2359296 | tf_op jit(solution)/shard_map/all_gather | solution.py:976
  88.0 3.3 copy-start.3
  91.3 1.8 copy-start.10
  92.5 2.8 copy-start.15
  92.6 56.1 %all-gather.8.cloned.1.call-start = ((), (), s32[]{:S(2)}) async-start(), calls=%async_computation.4 | async-start | bytes 2359296 | tf_op jit(solution)/shard_map/all_gather | solution.py:982
  96.2 3.3 copy-start.12
  120.0 8.8 %copy-start.17 = (bf16[512,1536]{1,0:T(8,128)(2,1)S(1)}, bf16[512,1536]{1,0:T(8,128)(2,1)}, u32[]{:S(2)}) copy-start(bf16[512,1536]{1,0:T(8,128)(2,1)} %all-gather.6.cloned.1.call-done.refs_2_) | copy-start | bytes 4718596
  159.0 8.1 %copy-start.22 = (bf16[512,2048]{1,0:T(8,128)(2,1)}, bf16[512,2048]{1,0:T(8,128)(2,1)S(1)}, u32[]{:S(2)}) copy-start(bf16[512,2048]{1,0:T(8,128)(2,1)S(1)} %get-tuple-element.36.refs_3_) | copy-start | bytes 6291460
  159.0 8.1 %copy-start.23 = (bf16[512,2048]{1,0:T(8,128)(2,1)}, bf16[512,2048]{1,0:T(8,128)(2,1)S(1)}, u32[]{:S(2)}) copy-start(bf16[512,2048]{1,0:T(8,128)(2,1)S(1)} %get-tuple-element.37.refs_0_) | copy-start | bytes 6291460
  159.0 15.5 %copy-start.21 = (bf16[512,2048]{1,0:T(8,128)(2,1)}, bf16[512,2048]{1,0:T(8,128)(2,1)S(1)}, u32[]{:S(2)}) copy-start(bf16[512,2048]{1,0:T(8,128)(2,1)S(1)} %get-tuple-element.35.refs_4_) | copy-start | bytes 6291460
  159.1 15.5 %slice-start.4 = ((s8[6291456]{0:T(1024)(128)(4,1)}), s8[4194304]{0:T(1024)(128)(4,1)S(1)}, s32[]{:S(2)}) async-start(s8[6291456]{0:T(1024)(128)(4,1)} %bitcast.86), calls=%async_computation.9 | async-start | bytes 8388608
  167.1 7.5 %slice-start.5 = ((s8[6291456]{0:T(1024)(128)(4,1)}), s8[2097152]{0:T(1024)(128)(4,1)S(1)}, s32[]{:S(2)}) async-start(s8[6291456]{0:T(1024)(128)(4,1)} %bitcast.86), calls=%async_computation.10 | async-start | bytes 4194304
  462.2 4.5 copy-start
  462.2 8.4 %copy-start.2 = (bf16[1536,2048]{1,0:T(8,128)(2,1)S(1)}, bf16[1536,2048]{1,0:T(8,128)(2,1)}, u32[]{:S(2)}) copy-start(bf16[1536,2048]{1,0:T(8,128)(2,1)} %get-tuple-element.25) | copy-start | bytes 18874372
  466.7 2.7 copy-start.13
  466.7 10.2 %slice-start.2 = ((s8[6291456]{0:T(1024)(128)(4,1)}), s8[4194304]{0:T(1024)(128)(4,1)S(1)}, s32[]{:S(2)}) async-start(s8[6291456]{0:T(1024)(128)(4,1)} %bitcast.75), calls=%async_computation.7 | async-start | bytes 8388608
  470.6 6.3 %slice-start.3 = ((s8[6291456]{0:T(1024)(128)(4,1)}), s8[2097152]{0:T(1024)(128)(4,1)S(1)}, s32[]{:S(2)}) async-start(s8[6291456]{0:T(1024)(128)(4,1)} %bitcast.75), calls=%async_computation.8 | async-start | bytes 4194304
  470.6 12.6 %slice-start = ((s8[6291456]{0:T(1024)(128)(4,1)}), s8[4194304]{0:T(1024)(128)(4,1)S(1)}, s32[]{:S(2)}) async-start(s8[6291456]{0:T(1024)(128)(4,1)} %bitcast.73), calls=%async_computation.5 | async-start | bytes 8388608
  476.9 6.3 %slice-start.1 = ((s8[6291456]{0:T(1024)(128)(4,1)}), s8[2097152]{0:T(1024)(128)(4,1)S(1)}, s32[]{:S(2)}) async-start(s8[6291456]{0:T(1024)(128)(4,1)} %bitcast.73), calls=%async_computation.6 | async-start | bytes 4194304
  483.2 6.6 %copy-start.4 = (bf16[768,1536]{1,0:T(8,128)(2,1)S(1)}, bf16[768,1536]{1,0:T(8,128)(2,1)}, u32[]{:S(2)}) copy-start(bf16[768,1536]{1,0:T(8,128)(2,1)} %get-tuple-element.24) | copy-start | bytes 7077892
  489.8 5.5 %copy-start.7 = (bf16[256,1536]{1,0:T(8,128)(2,1)S(1)}, bf16[256,1536]{1,0:T(8,128)(2,1)}, u32[]{:S(2)}) copy-start(bf16[256,1536]{1,0:T(8,128)(2,1)} %get-tuple-element.64) | copy-start | bytes 2359300
  492.6 3.5 copy-start.6
Sparse Core Ops, SparseCore 0:
  11.0 29.8 all-gather.3
  61.9 26.0 reduce-scatter.1
  92.7 27.2 all-gather.5
  121.4 27.2 all-gather.7
